TPU v7x, 256 devices: a whole 4x4x8 slice. The times are simulated.
256 devices in a mesh: band: 8 (over y, x_lo), mesh: 32 (over x_hi, z, core).
Axes of the slice: x: 4 (x_hi: 2, x_lo: 2; x = x_hi * 2 + x_lo), y: 4, z: 8, core: 2. Of those that a mesh axis runs over, the one named last changes fastest.
Arguments:
- bands_in: float32 [32768, 2048], P('mesh', 'band'), may hold values from -6 to 6
- cell_ham: float32 [96, 512, 512], P('mesh'), may hold values from -0.25 to 0.25
- cell_nodes: int32 [96, 512], P('mesh'), may hold values from 0 to 1023
- left_face: int32 [32, 128], P('mesh'), may hold values from 0 to 1023, as said below
- right_face: int32 [32, 128], P('mesh'), may hold values from 0 to 1023, as said below
- proj_values: float32 [1024, 18, 128], P('mesh'), may hold values from -0.375 to 0.375
- proj_nodes: int32 [1024, 128], P('mesh'), may hold values from 0 to 1023
- slot_owner: int32 [1024, 1], P('mesh'), may hold values from 0 to 31; in each aligned block of 32 rows (0 to 31, 32 to 63, ...) at most 2 rows name the same one
- slot_atom: int32 [1024], P('mesh'), may hold values from 0 to 15
- coupling: float32 [512, 18, 18], P('mesh'), may hold values from -1.5 to 1.5
- node_weight: float32 [32768], P('mesh'), may hold values from 0.00012207031 to 0.0012207031
- filter_center: float32 [1], replicated, may hold values from 0.5 to 1.5
- filter_half: float32 [1], replicated, may hold values from 2 to 3
Outputs:
- filtered: float32 [32768, 2048], P('mesh', 'band')
- margin: float32 [2048, 2048], P('band', 'mesh')
Inputs may be any that keep to these rules, and one draw needn't show every extreme that they name: `cell_nodes`: local node numbers within the cell's part. In each part the 128 entries of left_face and of right_face are all distinct and the two lists share no node; entry i of part p's right_face is the node that entry i of part p + 1's left_face names. `right_face`: see left_face. `proj_nodes`: local node numbers within the slot's part. `slot_owner`: among the 32 slots of one part, at most 2 name the same owner.
All inputs are finite; a program needn't handle non-finite values.
Results may differ from a plain program's by a relative error of at most 0.0002.
Values sent between devices are 32-bit elements; how exact they have to be, the bound alone decides.
A program may use at most 64 MiB of HBM per device.

v0:
```python
import jax
import jax.numpy as jnp
from jax import lax
from jax.sharding import PartitionSpec as P

precise = lax.Precision.HIGHEST


def shifted(value, axis, steps):
    count = lax.axis_size(axis)
    initial, last = (max(0, -steps), min(count, count - steps))
    return lax.ppermute(value, axis, [(source, source + steps) for source in range(initial, last)])


def passed_along(block, axis, distance):
    devices = range(lax.axis_size(axis))
    route = [((i - distance) % len(devices), i) for i in devices]
    return lax.ppermute(block, axis, route)


def cut_along(array, dim, count):
    lengths = array.shape
    parts = array.reshape(*lengths[:dim], count, lengths[dim] // count, *lengths[dim + 1 :])
    return jnp.moveaxis(parts, dim, 0)


def sum_at_owner(array, axis, dim):
    count = lax.axis_size(axis)
    parts = lax.all_to_all(cut_along(array, dim, count), axis, 0, 0, tiled=True)
    return jnp.sum(parts, axis=0)


def cell_apply(vectors, hamiltonians, node_lists):
    columns = vectors.shape[1]
    gathered = vectors[node_lists]
    product = jnp.einsum("cij,cjb->cib", hamiltonians, gathered, precision=precise)
    return jnp.zeros_like(vectors).at[node_lists.reshape(-1)].add(product.reshape(-1, columns))


def contract_rows(left_side, right_side):
    return lax.dot_general(left_side, right_side, (((0,), (0,)), ((), ())), precision=precise)


def per_device(
    bands_in,
    cell_ham,
    cell_nodes,
    left_face,
    right_face,
    proj_values,
    proj_nodes,
    slot_owner,
    slot_atom,
    coupling,
    node_weight,
    filter_center,
    filter_half,
):
    partitions = lax.axis_size("mesh")
    slot_count = proj_values.shape[0]
    projectors = proj_values.shape[1]
    owned_atoms = coupling.shape[0]
    columns = bands_in.shape[1]
    capacity = max(2, 2 * slot_count // partitions)
    owners = slot_owner[:, 0]
    matching = owners[:, None] == owners[None, :]
    ordinal = jnp.arange(slot_count)
    earlier = ordinal[None, :] < ordinal[:, None]
    position = jnp.sum(matching & earlier, axis=1)
    bucket = owners * capacity + position
    placing_mask = jnp.arange(partitions * capacity)[:, None] == bucket[None, :]
    placing = placing_mask.astype(jnp.float32)
    labels = jnp.sum(jnp.where(placing_mask, slot_atom[None, :] + 1, 0), axis=1).reshape(
        partitions, capacity
    )
    left_rows = left_face[0]
    right_rows = right_face[0]
    centre_value = filter_center[0]
    half_width = filter_half[0]
    flat_width = projectors * columns

    def nonlocal_term(vectors):
        selected = vectors[proj_nodes]
        coefficient = jnp.einsum("spn,snb->spb", proj_values, selected, precision=precise).reshape(
            slot_count, flat_width
        )
        outgoing = jnp.dot(placing, coefficient, precision=precise).reshape(
            partitions, capacity, flat_width
        )
        received, sources = (
            lax.all_to_all(outgoing, "mesh", split_axis=0, concat_axis=0, tiled=True),
            lax.all_to_all(labels, "mesh", split_axis=0, concat_axis=0, tiled=True),
        )
        membership = (jnp.arange(owned_atoms)[:, None] + 1 == sources.reshape(-1)[None, :]).astype(
            jnp.float32
        )
        totals = jnp.dot(
            membership, received.reshape(partitions * capacity, flat_width), precision=precise
        )
        totals = totals.reshape(owned_atoms, projectors, columns)
        applied = jnp.einsum("apq,aqb->apb", coupling, totals, precision=precise).reshape(
            owned_atoms, flat_width
        )
        returning = contract_rows(membership, applied).reshape(partitions, capacity, flat_width)
        answered = lax.all_to_all(returning, "mesh", split_axis=0, concat_axis=0, tiled=True)
        returned = contract_rows(placing, answered.reshape(partitions * capacity, flat_width))
        returned = returned.reshape(slot_count, projectors, columns)
        spreading = jnp.einsum("spn,spb->snb", proj_values, returned, precision=precise)
        return (
            jnp.zeros_like(vectors).at[proj_nodes.reshape(-1)].add(spreading.reshape(-1, columns))
        )

    def scaled(vectors):
        cell_part = cell_apply(vectors, cell_ham, cell_nodes)
        from_right = shifted(cell_part[left_rows], "mesh", -1)
        from_left = shifted(cell_part[right_rows], "mesh", 1)
        assembled = cell_part.at[right_rows].add(from_right).at[left_rows].add(from_left)
        operator = assembled + nonlocal_term(vectors)
        return (operator - centre_value * vectors) / half_width

    first_term = scaled(bands_in)
    second = 2.0 * scaled(first_term) - bands_in
    filtered = 2.0 * scaled(second) - first_term
    weighted = filtered * node_weight[:, None]
    groups = lax.axis_size("band")
    reach_count = groups // 2
    blocks = [contract_rows(weighted, filtered)]
    for offset in range(1, reach_count + 1):
        partner = passed_along(filtered, "band", -offset)
        blocks.append(contract_rows(weighted, partner))
    mirrored = []
    for offset in range(1, groups - reach_count):
        mirrored.append(passed_along(blocks[offset].T, "band", offset))
    blocks = blocks + mirrored[::-1]
    row_block = jnp.roll(jnp.concatenate(blocks, axis=1), lax.axis_index("band") * columns, axis=1)
    margin = sum_at_owner(row_block, "mesh", 1)
    return (filtered, margin)


def solution(mesh):
    placed = (
        P("mesh", "band"),
        P("mesh", None, None),
        P("mesh", None),
        P("mesh", None),
        P("mesh", None),
        P("mesh", None, None),
        P("mesh", None),
        P("mesh", None),
        P("mesh"),
        P("mesh", None, None),
        P("mesh"),
        P(),
        P(),
    )
    return jax.shard_map(
        per_device,
        mesh=mesh,
        in_specs=placed,
        out_specs=(P("mesh", "band"), P("band", "mesh")),
        check_vma=False,
    )
```

profile of v0, /device:TPU:48, one launch (start us, length us, event | category | flops | bytes accessed | tf_op | source)
XLA Modules:
  0.0 732.8 jit_solution(15909558942585977622)
XLA Ops:
  3.1 11.2 %all-to-all-start = ((s32[32,1,2]{2,1,0:T(1,128)}), s32[32,1,2]{2,1,0:T(1,128)S(1)}, u32[]{:S(2)}, u32[]{:S(2)}) async-start(s32[32,1,2]{2,1,0:T(1,128)} %bitcast.11), calls=%async_computation | async-start | bytes 32768 | tf_op jit(solution)/shard_map/all_to_all | solution.py:92
  15.1 17.3 %gather_fusion.3 = f32[4096,256]{1,0:T(8,128)} fusion(f32[1024,256]{1,0:T(8,128)} %param.13, s32[4096]{0:T(1024)S(1)} %fusion.76), kind=kCustom, calls=%fused_computation.3 | custom fusion | bytes 8404992 | tf_op jit(solution)/shard_map/gather | solution.py:83
  32.4 5.5 convolution_bitcast_fusion.5
  43.6 9.9 %all-to-all-start.1 = ((f32[32,2,4608]{2,1,0:T(2,128)}), f32[32,2,4608]{2,1,0:T(2,128)}, u32[]{:S(2)}, u32[]{:S(2)}) async-start(f32[32,2,4608]{2,1,0:T(2,128)} %copy.99), calls=%async_computation.1 | async-start | bytes 2359296 | tf_op jit(solution)/shard_map/all_to_all | solution.py:91
  54.9 32.0 %all-to-all-done.1 = f32[32,2,4608]{2,1,0:T(2,128)} async-done(((f32[32,2,4608]{2,1,0:T(2,128)}), f32[32,2,4608]{2,1,0:T(2,128)}, u32[]{:S(2)}, u32[]{:S(2)}) %all-to-all-start.1) | async-done | bytes 1179680 | tf_op jit(solution)/shard_map/all_to_all | solution.py:91
  86.9 3.1 reshape.285
  99.5 4.8 all-to-all-start.2
  104.3 5.9 gather_fusion
  110.2 7.7 %convolution_bitcast_fusion.2 = f32[3,512,256]{1,2,0:T(8,128)} fusion(f32[3,512,256]{2,1,0:T(8,128)} %bitcast.139, f32[3,512,512]{2,1,0:T(8,128)S(1)} %copy-done), kind=kOutput, calls=%fused_computation.26 | convolution fusion | flops 2415919104 | bytes 6291456 | tf_op jit(solution)/shard_map/cij,cjb->cib/dot_general | solution.py:36
  117.9 3.1 copy.95
  121.0 10.2 %scatter_custom_fusion = f32[1024,256]{1,0:T(8,128)} fusion(s32[1536]{0:T(1024)S(1)} %fusion.103, f32[1536,256]{1,0:T(8,128)} %bitcast.150, f32[]{:T(128)} %constant.18.clone.1), kind=kCustom, calls=%fused_computation.85 | custom fusion | flops 393216 | bytes 1049088 | tf_op jit(solution)/shard_map/scatter-add | solution.py:37
  131.3 2.6 gather_fusion.1
  135.8 2.6 gather_fusion.2
  142.2 3.7 scatter_fusion
  145.9 4.3 scatter_fusion.1
  150.2 3.1 reshape.287
  155.1 5.4 fusion.32
  160.5 23.8 %scatter_custom_fusion.3 = f32[1024,256]{1,0:T(8,128)} fusion(s32[4096]{0:T(1024)S(1)} %bitcast.162, f32[4096,256]{1,0:T(8,128)} %bitcast.148, f32[]{:T(128)} %constant.18.clone.1), kind=kCustom, calls=%fused_computation.83 | custom fusion | flops 1048576 | bytes 1049088 | tf_op jit(solution)/shard_map/scatter-add | solution.py:110
  184.3 3.0 subtract_divide_fusion
  187.3 17.3 %gather_fusion.7 = f32[4096,256]{1,0:T(8,128)} fusion(f32[1024,256]{1,0:T(8,128)} %subtract_divide_fusion, s32[4096]{0:T(1024)S(1)} %fusion.76), kind=kCustom, calls=%fused_computation.7 | custom fusion | bytes 8404992 | tf_op jit(solution)/shard_map/gather | solution.py:83
  204.6 5.5 convolution_bitcast_fusion.4
  214.8 43.7 %all_to_all.46 = f32[32,2,4608]{2,1,0:T(2,128)} all-to-all(f32[32,2,4608]{2,1,0:T(2,128)S(1)} %copy.110), channel_id=1, replica_groups=mesh['band'=8,'mesh'=32] {'mesh'}, dimensions={0} | all-to-all | bytes 2359296 | tf_op jit(solution)/shard_map/all_to_all | solution.py:91
  258.5 3.1 reshape.291
  271.1 5.6 all-to-all-start.4
  276.7 5.9 gather_fusion.4
  282.6 7.7 %convolution_bitcast_fusion.1 = f32[3,512,256]{1,2,0:T(8,128)} fusion(f32[3,512,256]{2,1,0:T(8,128)} %bitcast.140, f32[3,512,512]{2,1,0:T(8,128)S(1)} %copy-done), kind=kOutput, calls=%fused_computation.25 | convolution fusion | flops 2415919104 | bytes 6291456 | tf_op jit(solution)/shard_map/cij,cjb->cib/dot_general | solution.py:36
  290.3 3.0 copy.108
  293.4 10.3 %scatter_custom_fusion.4 = f32[1024,256]{1,0:T(8,128)} fusion(s32[1536]{0:T(1024)S(1)} %fusion.103, f32[1536,256]{1,0:T(8,128)} %bitcast.152, f32[]{:T(128)} %constant.18.clone.1), kind=kCustom, calls=%fused_computation.81 | custom fusion | flops 393216 | bytes 1049088 | tf_op jit(solution)/shard_map/scatter-add | solution.py:37
  303.6 2.6 gather_fusion.5
  308.3 2.6 gather_fusion.6
  313.2 3.8 scatter_fusion.2
  317.5 4.1 scatter_fusion.3
  321.6 3.1 reshape.293
  326.5 5.4 fusion.30
  331.9 23.9 %scatter_custom_fusion.7 = f32[1024,256]{1,0:T(8,128)} fusion(s32[4096]{0:T(1024)S(1)} %bitcast.163, f32[4096,256]{1,0:T(8,128)} %bitcast.149, f32[]{:T(128)} %constant.18.clone.1), kind=kCustom, calls=%fused_computation.79 | custom fusion | flops 1048576 | bytes 1049088 | tf_op jit(solution)/shard_map/scatter-add | solution.py:110
  355.8 3.4 multiply_subtract_fusion.1
  359.2 17.3 %gather_fusion.11 = f32[4096,256]{1,0:T(8,128)} fusion(f32[1024,256]{1,0:T(8,128)} %multiply_subtract_fusion.1, s32[4096]{0:T(1024)S(1)} %fusion.76), kind=kCustom, calls=%fused_computation.11 | custom fusion | bytes 8404992 | tf_op jit(solution)/shard_map/gather | solution.py:83
  376.5 5.5 convolution_bitcast_fusion.3
  386.7 44.7 %all_to_all.47 = f32[32,2,4608]{2,1,0:T(2,128)} all-to-all(f32[32,2,4608]{2,1,0:T(2,128)S(1)} %copy.121), channel_id=1, replica_groups=mesh['band'=8,'mesh'=32] {'mesh'}, dimensions={0} | all-to-all | bytes 2359296 | tf_op jit(solution)/shard_map/all_to_all | solution.py:91
  431.4 3.1 reshape.297
  444.0 5.6 all-to-all-start.6
  449.7 5.9 gather_fusion.8
  455.6 7.7 %convolution_bitcast_fusion = f32[3,512,256]{1,2,0:T(8,128)} fusion(f32[3,512,256]{2,1,0:T(8,128)} %bitcast.138, f32[3,512,512]{2,1,0:T(8,128)S(1)} %copy-done), kind=kOutput, calls=%fused_computation.24 | convolution fusion | flops 2415919104 | bytes 6291456 | tf_op jit(solution)/shard_map/cij,cjb->cib/dot_general | solution.py:36
  463.3 3.0 copy.119
  466.3 10.3 %scatter_custom_fusion.8 = f32[1024,256]{1,0:T(8,128)} fusion(s32[1536]{0:T(1024)S(1)} %fusion.103, f32[1536,256]{1,0:T(8,128)} %bitcast.151, f32[]{:T(128)} %constant.18.clone.1), kind=kCustom, calls=%fused_computation.77 | custom fusion | flops 393216 | bytes 1049088 | tf_op jit(solution)/shard_map/scatter-add | solution.py:37
  476.6 2.6 gather_fusion.9
  481.2 2.6 gather_fusion.10
  486.1 3.8 scatter_fusion.4
  490.4 3.9 scatter_fusion.5
  494.4 3.1 reshape.299
  499.3 5.4 fusion.28
  504.7 23.8 %scatter_custom_fusion.11 = f32[1024,256]{1,0:T(8,128)} fusion(s32[4096]{0:T(1024)S(1)} %bitcast.164, f32[4096,256]{1,0:T(8,128)} %bitcast.147, f32[]{:T(128)} %constant.18.clone.1), kind=kCustom, calls=%fused_computation.75 | custom fusion | flops 1048576 | bytes 1049088 | tf_op jit(solution)/shard_map/scatter-add | solution.py:110
  528.5 3.4 multiply_subtract_fusion
  532.9 3.9 collective-permute-start.8
  537.8 4.3 constant_dynamic-update-slice_fusion.15
  542.1 16.2 %collective-permute-done.6 = f32[1024,256]{1,0:T(8,128)} collective-permute-done((f32[1024,256]{1,0:T(8,128)}, f32[1024,256]{1,0:T(8,128)}, u32[]{:S(2)}, u32[]{:S(2)}) %collective-permute-start.6) | collective-permute-done | bytes 1048608 | tf_op jit(solution)/shard_map/ppermute | solution.py:18
  558.3 4.2 constant_dynamic-update-slice_fusion.14
  562.5 4.3 constant_dynamic-update-slice_fusion.13
  566.8 14.6 %collective-permute-done.8 = f32[1024,256]{1,0:T(8,128)} collective-permute-done((f32[1024,256]{1,0:T(8,128)}, f32[1024,256]{1,0:T(8,128)}, u32[]{:S(2)}, u32[]{:S(2)}) %collective-permute-start.8) | collective-permute-done | bytes 1048608 | tf_op jit(solution)/shard_map/ppermute | solution.py:18
  581.5 4.3 constant_dynamic-update-slice_fusion.12
  587.6 51.8 %collective-permute-start.10 = (f32[256,256]{0,1:T(8,128)}, f32[256,256]{0,1:T(8,128)}, u32[]{:S(2)}, u32[]{:S(2)}) collective-permute-start(f32[256,256]{0,1:T(8,128)} %bitcast.153), channel_id=1, source_target_pairs={{160,0},{192,32},{224,64},{0,96},{32,128},{64,160},{96,192},{128,2... | collective-permute-start | bytes 786440 | tf_op jit(solution)/shard_map/ppermute | solution.py:18
  642.8 4.3 constant_dynamic-update-slice_fusion.11
  648.8 6.9 collective-permute-done.11
  667.6 62.6 %all_to_all.48 = f32[32,256,64]{1,2,0:T(8,128)} all-to-all(f32[32,256,64]{1,2,0:T(8,128)S(1)} %bitcast.137), channel_id=1, replica_groups=mesh['band'=8,'mesh'=32] {'mesh'}, dimensions={0} | all-to-all | bytes 4194304 | tf_op jit(solution)/shard_map/all_to_all | solution.py:29
  (108 shorter events, 90.6 us)
Async XLA Ops:
  0.6 109.6 %copy-start = (f32[3,512,512]{2,1,0:T(8,128)S(1)}, f32[3,512,512]{2,1,0:T(8,128)}, u32[]{:S(2)}) copy-start(f32[3,512,512]{2,1,0:T(8,128)} %param.14) | copy-start | bytes 9437188
  3.1 40.5 %all-to-all-start = ((s32[32,1,2]{2,1,0:T(1,128)}), s32[32,1,2]{2,1,0:T(1,128)S(1)}, u32[]{:S(2)}, u32[]{:S(2)}) async-start(s32[32,1,2]{2,1,0:T(1,128)} %bitcast.11), calls=%async_computation | async-start | bytes 32768 | tf_op jit(solution)/shard_map/all_to_all | solution.py:92
  15.1 17.3 %copy-start.1 = (f32[32,18,128]{2,0,1:T(8,128)S(1)}, f32[32,18,128]{2,0,1:T(8,128)}, u32[]{:S(2)}) copy-start(f32[32,18,128]{2,0,1:T(8,128)} %param.18) | copy-start | bytes 884740
  43.6 43.2 %all-to-all-start.1 = ((f32[32,2,4608]{2,1,0:T(2,128)}), f32[32,2,4608]{2,1,0:T(2,128)}, u32[]{:S(2)}, u32[]{:S(2)}) async-start(f32[32,2,4608]{2,1,0:T(2,128)} %copy.99), calls=%async_computation.1 | async-start | bytes 2359296 | tf_op jit(solution)/shard_map/all_to_all | solution.py:91
  97.5 6.7 copy-start.7
  99.5 50.7 %all-to-all-start.2 = ((f32[32,2,4608]{2,1,0:T(2,128)}), f32[32,2,4608]{2,1,0:T(2,128)}, u32[]{:S(2)}, u32[]{:S(2)}) async-start(f32[32,2,4608]{2,1,0:T(2,128)} %copy.103), calls=%async_computation.2 | async-start | bytes 2359296 | tf_op jit(solution)/shard_map/all_to_all | solution.py:105
  117.9 13.3 %copy-start.8 = (s32[1,128]{1,0:T(1,128)S(1)}, s32[1,128]{1,0:T(1,128)}, u32[]{:S(2)}) copy-start(s32[1,128]{1,0:T(1,128)} %param.17) | copy-start | bytes 1540
  117.9 13.3 %copy-start.9 = (s32[1,128]{1,0:T(1,128)S(1)}, s32[1,128]{1,0:T(1,128)}, u32[]{:S(2)}) copy-start(s32[1,128]{1,0:T(1,128)} %param.16) | copy-start | bytes 1540
  120.9 19.9 %copy-start.6 = (s32[32,128]{1,0:T(8,128)S(1)}, s32[32,128]{1,0:T(8,128)}, u32[]{:S(2)}) copy-start(s32[32,128]{1,0:T(8,128)} %param.19) | copy-start | bytes 49156
  133.9 8.3 %collective-permute-start = (f32[128,256]{1,0:T(8,128)}, f32[128,256]{1,0:T(8,128)}, u32[]{:S(2)}, u32[]{:S(2)}) collective-permute-start(f32[128,256]{1,0:T(8,128)} %gather_fusion.1), channel_id=1, source_target_pairs={{1,0},{2,1},{3,2},{4,3},{5,4},{6,5},{7,6},{8,7},{9,8},{10,9},{11,1... | collective-permute-start | bytes 393224 | tf_op jit(solution)/shard_map/ppermute | solution.py:12
  138.4 7.5 %collective-permute-start.1 = (f32[128,256]{1,0:T(8,128)}, f32[128,256]{1,0:T(8,128)}, u32[]{:S(2)}, u32[]{:S(2)}) collective-permute-start(f32[128,256]{1,0:T(8,128)} %gather_fusion.2), channel_id=1, source_target_pairs={{0,1},{1,2},{2,3},{3,4},{4,5},{5,6},{6,7},{7,8},{8,9},{9,10},{10,1... | collective-permute-start | bytes 393224 | tf_op jit(solution)/shard_map/ppermute | solution.py:12
  271.1 50.5 %all-to-all-start.4 = ((f32[32,2,4608]{2,1,0:T(2,128)}), f32[32,2,4608]{2,1,0:T(2,128)}, u32[]{:S(2)}, u32[]{:S(2)}) async-start(f32[32,2,4608]{2,1,0:T(2,128)} %copy.114), calls=%async_computation.4 | async-start | bytes 2359296 | tf_op jit(solution)/shard_map/all_to_all | solution.py:105
  306.2 7.0 collective-permute-start.2
  310.9 6.6 collective-permute-start.3
  444.0 50.3 %all-to-all-start.6 = ((f32[32,2,4608]{2,1,0:T(2,128)}), f32[32,2,4608]{2,1,0:T(2,128)}, u32[]{:S(2)}, u32[]{:S(2)}) async-start(f32[32,2,4608]{2,1,0:T(2,128)} %copy.125), calls=%async_computation.6 | async-start | bytes 2359296 | tf_op jit(solution)/shard_map/all_to_all | solution.py:105
  479.2 7.0 collective-permute-start.4
  483.8 6.6 collective-permute-start.5
  528.5 9.3 %copy-start.5 = (f32[1024]{0:T(1024)S(1)}, f32[1024]{0:T(1024)}, u32[]{:S(2)}) copy-start(f32[1024]{0:T(1024)} %param.23) | copy-start | bytes 12292
  531.9 26.3 %collective-permute-start.6 = (f32[1024,256]{1,0:T(8,128)}, f32[1024,256]{1,0:T(8,128)}, u32[]{:S(2)}, u32[]{:S(2)}) collective-permute-start(f32[1024,256]{1,0:T(8,128)} %multiply_subtract_fusion), channel_id=1, source_target_pairs={{32,0},{64,32},{96,64},{128,96},{160,128},{192,160},{224,192},{0,2... | collective-permute-start | bytes 3145736 | tf_op jit(solution)/shard_map/ppermute | solution.py:18
  532.4 30.1 %collective-permute-start.7 = (f32[1024,256]{1,0:T(8,128)}, f32[1024,256]{1,0:T(8,128)}, u32[]{:S(2)}, u32[]{:S(2)}) collective-permute-start(f32[1024,256]{1,0:T(8,128)} %multiply_subtract_fusion), channel_id=1, source_target_pairs={{64,0},{96,32},{128,64},{160,96},{192,128},{224,160},{0,192},{32,2... | collective-permute-start | bytes 3145736 | tf_op jit(solution)/shard_map/ppermute | solution.py:18
  532.9 48.6 %collective-permute-start.8 = (f32[1024,256]{1,0:T(8,128)}, f32[1024,256]{1,0:T(8,128)}, u32[]{:S(2)}, u32[]{:S(2)}) collective-permute-start(f32[1024,256]{1,0:T(8,128)} %multiply_subtract_fusion), channel_id=1, source_target_pairs={{96,0},{128,32},{160,64},{192,96},{224,128},{0,160},{32,192},{64,2... | collective-permute-start | bytes 3145736 | tf_op jit(solution)/shard_map/ppermute | solution.py:18
  536.7 106.0 %collective-permute-start.9 = (f32[1024,256]{1,0:T(8,128)}, f32[1024,256]{1,0:T(8,128)}, u32[]{:S(2)}, u32[]{:S(2)}) collective-permute-start(f32[1024,256]{1,0:T(8,128)} %multiply_subtract_fusion), channel_id=1, source_target_pairs={{128,0},{160,32},{192,64},{224,96},{0,128},{32,160},{64,192},{96,2... | collective-permute-start | bytes 3145736 | tf_op jit(solution)/shard_map/ppermute | solution.py:18
  587.6 59.5 %collective-permute-start.10 = (f32[256,256]{0,1:T(8,128)}, f32[256,256]{0,1:T(8,128)}, u32[]{:S(2)}, u32[]{:S(2)}) collective-permute-start(f32[256,256]{0,1:T(8,128)} %bitcast.153), channel_id=1, source_target_pairs={{160,0},{192,32},{224,64},{0,96},{32,128},{64,160},{96,192},{128,2... | collective-permute-start | bytes 786440 | tf_op jit(solution)/shard_map/ppermute | solution.py:18
  641.2 14.5 %collective-permute-start.11 = (f32[256,256]{0,1:T(8,128)}, f32[256,256]{0,1:T(8,128)}, u32[]{:S(2)}, u32[]{:S(2)}) collective-permute-start(f32[256,256]{0,1:T(8,128)} %bitcast.154), channel_id=1, source_target_pairs={{192,0},{224,32},{0,64},{32,96},{64,128},{96,160},{128,192},{160,2... | collective-permute-start | bytes 786440 | tf_op jit(solution)/shard_map/ppermute | solution.py:18
  642.1 15.4 %collective-permute-start.12 = (f32[256,256]{0,1:T(8,128)}, f32[256,256]{0,1:T(8,128)S(1)}, u32[]{:S(2)}, u32[]{:S(2)}) collective-permute-start(f32[256,256]{0,1:T(8,128)} %bitcast.155), channel_id=1, source_target_pairs={{224,0},{0,32},{32,64},{64,96},{96,128},{128,160},{160,192},{192,2... | collective-permute-start | bytes 786440 | tf_op jit(solution)/shard_map/ppermute | solution.py:18
  642.8 15.4 %copy-start.4 = (f32[256,256]{0,1:T(8,128)S(1)}, f32[256,256]{0,1:T(8,128)}, u32[]{:S(2)}) copy-start(f32[256,256]{0,1:T(8,128)} %get-tuple-element.3) | copy-start | bytes 786436
  642.8 16.8 %copy-start.2 = (f32[256,256]{0,1:T(8,128)S(1)}, f32[256,256]{0,1:T(8,128)}, u32[]{:S(2)}) copy-start(f32[256,256]{0,1:T(8,128)} %get-tuple-element.7) | copy-start | bytes 786436
  647.1 13.3 %copy-start.3 = (f32[256,256]{0,1:T(8,128)S(1)}, f32[256,256]{0,1:T(8,128)}, u32[]{:S(2)}) copy-start(f32[256,256]{0,1:T(8,128)} %get-tuple-element.9) | copy-start | bytes 786436
where the time goes:
time: 743 us; the launch traced here: 733 us
  local copies, waits for them, and re-layouts  154 us (21%)
  blocking collectives  151 us (20%)
  other arithmetic  141 us (19%)
  starting transfers between devices  108 us (15%)
  matrix products  105 us (14%)
  waiting for transfers between devices  70.8 us (10%)
    all_to_all x2, blocking collectives, nonlocal_term(): lax.all_to_all(outgoing, 'mesh', split_axis=0, concat_axis=0, tiled=True)  88.4 us
    scatter-add x3, other arithmetic, nonlocal_term(): jnp.zeros_like(vectors).at[proj_nodes.reshape(-1)]  71.5 us
    all_to_all x1, blocking collectives, sum_at_owner(): parts = lax.all_to_all(cut_along(array, dim, count), axis, 0, 0, tiled=True)  62.6 us
    ppermute x7, starting transfers between devices, passed_along(): return lax.ppermute(block, axis, route)  58.4 us
    gather x3, local copies, waits for them, and re-layouts, nonlocal_term(): selected = vectors[proj_nodes]  51.9 us
    ppermute x7, waiting for transfers between devices, passed_along(): return lax.ppermute(block, axis, route)  37.8 us
    dot_general x11, matrix products, contract_rows(): lax.dot_general(left_side, right_side, (((0,), (0,)), ((), ())), precisio...  32 us
    all_to_all x1, waiting for transfers between devices, nonlocal_term(): lax.all_to_all(outgoing, 'mesh', split_axis=0, concat_axis=0, tiled=True)  32 us
  transfers between devices with their start and end apart: 18, of which 6 were waited for; matrix products, arithmetic and copies ran while one was open for 25% of the time, Pallas kernels for 0%

commit v1 on v0

v1 whole, which is shorter than its diff:
```python
import functools

import jax
import jax.numpy as jnp
from jax import lax
from jax.experimental import pallas as pl
from jax.experimental.pallas import tpu as pltpu
from jax.sharding import PartitionSpec as P

MESH = pl.DeviceIdType.MESH
precise = lax.Precision.HIGHEST
f32, bf16, i32 = jnp.float32, jnp.bfloat16, jnp.int32

PARTS = 32
NODES = 1024
COLS = 256
SLOTS = 32
PROJ = 18
PADDED = 24
ATOMS = 16
CELLS = 3
CELL = 512
FACE = 128
MAIN = PARTS * 32
ROWS = MAIN + PARTS * 8
TERMS = ATOMS * PADDED
BLOCK = 256


def mm(a, b):
    return jnp.dot(a, b, preferred_element_type=f32)


def split(x):
    high = x.astype(bf16)
    return high, (x - high.astype(f32)).astype(bf16)


def iota(shape, dim):
    return lax.broadcasted_iota(i32, shape, dim)


def hot(mask):
    return jnp.where(mask, 1.0, 0.0).astype(bf16)


def rows_at(index, size=BLOCK):
    return pl.ds(pl.multiple_of(index * size, size), size)


def loop(count, body):
    def step(i, carry):
        body(i)
        return carry

    lax.fori_loop(0, count, step, 0)


def filter_kernel(
    scalars,
    bands_in,
    cell_ham,
    cell_rows,
    cell_cols,
    face_row,
    face_col,
    proj_values,
    proj_cols,
    row_source,
    labels,
    coupling,
    filtered,
    b24,
    b24h,
    b24l,
    b8h,
    b8l,
    bth,
    btl,
    gat,
    sca,
    fgat,
    fsca,
    member,
    memt,
    cbh,
    cbl,
    vh,
    vl,
    xh,
    xl,
    gh,
    gl,
    ph,
    plo,
    cells,
    previous,
    out1,
    in1,
    out2,
    in2,
    lab_in,
    face_out,
    face_in,
    s1,
    r1,
    s2,
    r2,
    sl,
    rl,
    sf,
    rf,
):
    me = lax.axis_index("mesh")
    band = lax.axis_index("band")
    centre, half = scalars[0, 0], scalars[0, 1]

    def peer(k):
        return lax.rem(me + k, PARTS)

    face_in[...] = jnp.zeros_like(face_in)
    barrier = pltpu.get_barrier_semaphore()

    def greet(k):
        pl.semaphore_signal(barrier, inc=1, device_id=(band, peer(k + 1)), device_id_type=MESH)

    loop(PARTS - 1, greet)

    b24[...] = jnp.zeros_like(b24)
    for s in range(SLOTS):
        spread = hot(proj_cols[:, s : s + 1] == iota((128, NODES), 1))
        high, low = split(proj_values[s])
        b24[s * PADDED : s * PADDED + PROJ, :] = mm(high, spread) + mm(low, spread)
    high, low = split(b24[...])
    b24h[...] = high
    b24l[...] = low

    def place(i):
        at = rows_at(i)
        chosen = hot(row_source[at, :] == iota((BLOCK, SLOTS * PADDED), 1))
        b8h[at, :] = mm(chosen, b24h[...]).astype(bf16)
        b8l[at, :] = mm(chosen, b24l[...]).astype(bf16)

    loop(ROWS // BLOCK, place)

    def set_field(x):
        high, low = split(x)
        vh[...] = high
        vl[...] = low

    filtered[...] = bands_in[...]
    previous[...] = bands_in[...]
    set_field(bands_in[...])

    def copy_to(source, target, send, receive, o):
        return pltpu.make_async_remote_copy(
            source.at[o],
            target.at[me],
            send.at[o],
            receive.at[me],
            device_id=(band, o),
            device_id_type=MESH,
        )

    def arrival(source, target, send, receive, q):
        return pltpu.make_async_remote_copy(
            source.at[q],
            target.at[q],
            send.at[q],
            receive.at[q],
            device_id=(band, q),
            device_id_type=MESH,
        )

    def exchange(rows_of, out, target, send, receive, wait=None):
        tail = rows_of(MAIN // BLOCK)
        first = lax.rem(iota((BLOCK, 128), 0), 8) < 4
        out[:, 64:72, :] = jnp.where(first, tail[:, :128], tail[:, 128:]).reshape(PARTS, 8, 128)

        def group(t):
            g = lax.rem(me // 8 + 1 + t, 4)
            block = rows_of(g)
            out[pl.ds(g * 8, 8), 0:32, :] = block[:, :128].reshape(8, 32, 128)
            out[pl.ds(g * 8, 8), 32:64, :] = block[:, 128:].reshape(8, 32, 128)

            def one(i):
                o = g * 8 + lax.rem(me + i, 8)

                @pl.when(o != me)
                def _():
                    copy_to(out, target, send, receive, o).start()

            loop(8, one)

        loop(4, group)
        target[me] = out[me]

    def collect(out, target, send, receive):
        def one(k):
            arrival(out, target, send, receive, peer(k + 1)).wait_recv()

        loop(PARTS - 1, one)
        main = target[:, 0:64, :]
        left = main[:, 0:32, :].reshape(MAIN, 128)
        right = main[:, 32:64, :].reshape(MAIN, 128)
        tail = target[:, 64:72, :].reshape(BLOCK, 128)
        first = lax.rem(iota((BLOCK, 128), 0), 8) < 4
        for columns, top, keep in ((0, left, first), (128, right, jnp.logical_not(first))):
            high, low = split(top)
            xh[0:MAIN, columns : columns + 128] = high
            xl[0:MAIN, columns : columns + 128] = low
            high, low = split(jnp.where(keep, tail, 0.0))
            xh[MAIN:ROWS, columns : columns + 128] = high
            xl[MAIN:ROWS, columns : columns + 128] = low

    def sent(out, target, send, receive):
        def one(k):
            arrival(out, target, send, receive, peer(k + 1)).wait_send()

        loop(PARTS - 1, one)

    def coefficient(i):
        at = rows_at(i)
        return mm(b8h[at, :], vh[...]) + (mm(b8h[at, :], vl[...]) + mm(b8l[at, :], vh[...]))

    pl.semaphore_wait(barrier, PARTS - 1)

    def tell(k):
        copy_to(labels, lab_in, sl, rl, peer(k + 1)).start()

    loop(PARTS - 1, tell)
    exchange(coefficient, out1, in1, s1, r1)
    lab_in[me] = labels[me]

    for c in range(CELLS):
        for h in range(2):
            gat[c * CELL + h * BLOCK : c * CELL + (h + 1) * BLOCK, :] = hot(
                cell_cols[h * BLOCK : (h + 1) * BLOCK, c : c + 1] == iota((BLOCK, NODES), 1)
            )
    for i in range(NODES // BLOCK):
        row = iota((BLOCK, CELL), 0) + i * BLOCK
        for c in range(CELLS):
            sca[i * BLOCK : (i + 1) * BLOCK, c * CELL : (c + 1) * CELL] = hot(row == cell_rows[c : c + 1, :])
        fsca[i * BLOCK : (i + 1) * BLOCK, :] = hot(row[:, :256] == face_row[...])
    fgat[...] = hot(face_col[...] == iota((2 * FACE, NODES), 1))
    for i in range(ROWS // BLOCK):
        at = slice(i * BLOCK, (i + 1) * BLOCK)
        bth[:, at] = b8h[at, :].astype(f32).T.astype(bf16)
        btl[:, at] = b8l[at, :].astype(f32).T.astype(bf16)
    repeat = hot(iota((PADDED, TERMS), 0) == lax.rem(iota((PADDED, TERMS), 1), PADDED))
    same = iota((TERMS, TERMS), 0) // PADDED == iota((TERMS, TERMS), 1) // PADDED
    high, low = split(coupling[...])
    cbh[...] = jnp.where(same, mm(high, repeat), 0.0).astype(bf16)
    cbl[...] = jnp.where(same, mm(low, repeat), 0.0).astype(bf16)

    def told(k):
        arrival(labels, lab_in, sl, rl, peer(k + 1)).wait()

    loop(PARTS - 1, told)
    col = iota((128, ROWS), 1)
    index = jnp.where(col < MAIN, lax.rem(col, 32), 32 + lax.rem(col, 8))
    place_of = hot(iota((128, ROWS), 0) == index)
    named = mm(lab_in[...].reshape(PARTS * 8, 128).astype(bf16), place_of)
    col = iota((PARTS * 8, ROWS), 1)
    source = jnp.where(col < MAIN, col // 32, (col - MAIN) // 8)
    atom = jnp.sum(jnp.where(iota((PARTS * 8, ROWS), 0) == source * 8, named, 0.0), axis=0, keepdims=True)
    col = iota((1, ROWS), 1)
    number = jnp.where(col < MAIN, lax.rem(col, 32), 32 + lax.rem(col, 4))
    key = jnp.where(atom < 0.0, -1, atom.astype(i32) * PADDED + lax.rem(number, PROJ))
    for i in range(ROWS // BLOCK):
        at = slice(i * BLOCK, (i + 1) * BLOCK)
        mask = jnp.where(iota((TERMS, BLOCK), 0) == key[:, at], 1.0, 0.0)
        member[:, at] = mask.astype(bf16)
        memt[at, :] = mask.T.astype(bf16)

    def returned(i):
        at = rows_at(i)
        return mm(memt[at, :], ph[0:TERMS, :]) + mm(memt[at, :], plo[0:TERMS, :])

    def face_copy(step, low, other):
        source = face_out.at[pl.ds(0 if low else FACE, FACE)]
        target = face_in.at[step, pl.ds(FACE if low else 0, FACE)]
        side = 0 if low else 1
        return pltpu.make_async_remote_copy(
            source, target, sf.at[side], rf.at[step, 1 - side], device_id=(band, other), device_id_type=MESH
        )

    def face_wait(step, low, other):
        source = face_out.at[pl.ds(0 if low else FACE, FACE)]
        target = face_in.at[step, pl.ds(0 if low else FACE, FACE)]
        side = 0 if low else 1
        return pltpu.make_async_remote_copy(
            source, target, sf.at[side], rf.at[step, side], device_id=(band, other), device_id_type=MESH
        )

    def degree(step):
        gain = jnp.where(step == 0, 1.0, 2.0) / half
        keep = jnp.where(step == 0, 0.0, 1.0)

        def pick(i):
            at = rows_at(i)
            gh[at, :] = mm(gat[at, :], vh[...]).astype(bf16)
            gl[at, :] = mm(gat[at, :], vl[...]).astype(bf16)

        loop(CELLS * CELL // BLOCK, pick)

        def multiply(c):
            at = rows_at(c, CELL)
            for h in range(2):
                high, low = split(cell_ham[c, h * BLOCK : (h + 1) * BLOCK, :])
                result = mm(high, gh[at, :]) + (mm(high, gl[at, :]) + mm(low, gh[at, :]))
                high, low = split(result)
                to = pl.ds(pl.multiple_of(c * CELL + h * BLOCK, BLOCK), BLOCK)
                ph[to, :] = high
                plo[to, :] = low

        loop(CELLS, multiply)

        def add(i):
            at = rows_at(i)
            cells[at, :] = mm(sca[at, :], ph[...]) + mm(sca[at, :], plo[...])

        loop(NODES // BLOCK, add)
        high, low = split(cells[...])
        gh[0:NODES, :] = high
        gl[0:NODES, :] = low
        face_out[...] = mm(fgat[...], gh[0:NODES, :]) + mm(fgat[...], gl[0:NODES, :])

        @pl.when(me > 0)
        def _():
            face_copy(step, True, me - 1).start()

        @pl.when(me < PARTS - 1)
        def _():
            face_copy(step, False, me + 1).start()

        collect(out1, in1, s1, r1)
        totals = mm(member[...], xh[...]) + mm(member[...], xl[...])
        high, low = split(totals)
        applied = mm(cbh[...], high) + (mm(cbh[...], low) + mm(cbl[...], high))
        high, low = split(applied)
        ph[0:TERMS, :] = high
        plo[0:TERMS, :] = low
        exchange(returned, out2, in2, s2, r2)

        @pl.when(me > 0)
        def _():
            face_wait(step, True, me - 1).wait()

        @pl.when(me < PARTS - 1)
        def _():
            face_wait(step, False, me + 1).wait()

        high, low = split(face_in[step])
        gh[0 : 2 * FACE, :] = high
        gl[0 : 2 * FACE, :] = low

        def assemble(i):
            at = rows_at(i)
            summed = cells[at, :] + mm(fsca[at, :], gh[0:256, :]) + mm(fsca[at, :], gl[0:256, :])
            field = filtered[at, :]
            cells[at, :] = (summed - centre * field) * gain - keep * previous[at, :]
            previous[at, :] = field

        loop(NODES // BLOCK, assemble)
        sent(out1, in1, s1, r1)
        collect(out2, in2, s2, r2)

        def finish(i):
            at = rows_at(i)
            back = mm(bth[at, :], xh[...]) + (mm(bth[at, :], xl[...]) + mm(btl[at, :], xh[...]))
            field = cells[at, :] + gain * back
            filtered[at, :] = field
            high, low = split(field)
            vh[at, :] = high
            vl[at, :] = low

        loop(NODES // BLOCK, finish)
        sent(out2, in2, s2, r2)

        @pl.when(step < 2)
        def _():
            exchange(coefficient, out1, in1, s1, r1)

    loop(3, degree)


def run_filter(scalars, bands_in, cell_ham, cell_nodes, left_face, right_face, proj_values, proj_nodes, slot_owner, slot_atom, coupling):
    owners = slot_owner[:, 0]
    ordinal = jnp.arange(SLOTS)
    position = jnp.sum((owners[:, None] == owners[None, :]) & (ordinal[None, :] < ordinal[:, None]), axis=1)
    bucket = owners * 2 + position
    placed = jnp.arange(2 * PARTS)[:, None] == bucket[None, :]
    slot = jnp.sum(jnp.where(placed, ordinal[None, :] + 1, 0), axis=1) - 1
    label = jnp.sum(jnp.where(placed, slot_atom[None, :] + 1, 0), axis=1) - 1
    slot, label = slot.reshape(PARTS, 2), label.reshape(PARTS, 2)
    lane = jnp.arange(128)
    labels = jnp.where(lane[None, :] < PROJ, label[:, :1], jnp.where(lane[None, :] < 40, label[:, 1:], -1))
    labels = jnp.broadcast_to(labels.astype(f32)[:, None, :], (PARTS, 8, 128))
    number = jnp.concatenate([jnp.arange(32), 32 + jnp.arange(8) % 4])
    taken = jnp.where(number[None, :] < PROJ, slot[:, :1], slot[:, 1:])
    source = jnp.where(taken < 0, -1, taken * PADDED + number[None, :] % PROJ)
    row_source = jnp.concatenate([source[:, :32].reshape(-1), source[:, 32:].reshape(-1)])[:, None]
    faces = jnp.concatenate([left_face, right_face], axis=1)
    padded = jnp.pad(coupling, ((0, 0), (0, PADDED - PROJ), (0, PADDED - PROJ))).reshape(TERMS, PADDED)
    vmem = pl.BlockSpec(memory_space=pltpu.VMEM)
    D = pltpu.SemaphoreType.DMA
    V = pltpu.VMEM
    return pl.pallas_call(
        filter_kernel,
        out_shape=jax.ShapeDtypeStruct((NODES, COLS), f32),
        in_specs=[pl.BlockSpec(memory_space=pltpu.SMEM)] + [vmem] * 11,
        out_specs=vmem,
        scratch_shapes=[
            V((SLOTS * PADDED, NODES), f32),
            V((SLOTS * PADDED, NODES), bf16),
            V((SLOTS * PADDED, NODES), bf16),
            V((ROWS, NODES), bf16),
            V((ROWS, NODES), bf16),
            V((NODES, ROWS), bf16),
            V((NODES, ROWS), bf16),
            V((CELLS * CELL, NODES), bf16),
            V((NODES, CELLS * CELL), bf16),
            V((2 * FACE, NODES), bf16),
            V((NODES, 2 * FACE), bf16),
            V((TERMS, ROWS), bf16),
            V((ROWS, TERMS), bf16),
            V((TERMS, TERMS), bf16),
            V((TERMS, TERMS), bf16),
            V((NODES, COLS), bf16),
            V((NODES, COLS), bf16),
            V((ROWS, COLS), bf16),
            V((ROWS, COLS), bf16),
            V((CELLS * CELL, COLS), bf16),
            V((CELLS * CELL, COLS), bf16),
            V((CELLS * CELL, COLS), bf16),
            V((CELLS * CELL, COLS), bf16),
            V((NODES, COLS), f32),
            V((NODES, COLS), f32),
            V((PARTS, 72, 128), f32),
            V((PARTS, 72, 128), f32),
            V((PARTS, 72, 128), f32),
            V((PARTS, 72, 128), f32),
            V((PARTS, 8, 128), f32),
            V((2 * FACE, COLS), f32),
            V((3, 2 * FACE, COLS), f32),
            D((PARTS,)),
            D((PARTS,)),
            D((PARTS,)),
            D((PARTS,)),
            D((PARTS,)),
            D((PARTS,)),
            D((2,)),
            D((3, 2)),
        ],
        compiler_params=pltpu.CompilerParams(
            collective_id=0, has_side_effects=True, vmem_limit_bytes=58 * 2**20
        ),
        name="filter_bands",
    )(
        scalars,
        bands_in,
        cell_ham,
        cell_nodes,
        cell_nodes.T,
        faces,
        faces.T,
        proj_values,
        proj_nodes.T,
        row_source.astype(i32),
        labels,
        padded,
    )


def passed_along(block, axis, distance):
    devices = range(lax.axis_size(axis))
    route = [((i - distance) % len(devices), i) for i in devices]
    return lax.ppermute(block, axis, route)


def cut_along(array, dim, count):
    lengths = array.shape
    parts = array.reshape(*lengths[:dim], count, lengths[dim] // count, *lengths[dim + 1 :])
    return jnp.moveaxis(parts, dim, 0)


def sum_at_owner(array, axis, dim):
    count = lax.axis_size(axis)
    parts = lax.all_to_all(cut_along(array, dim, count), axis, 0, 0, tiled=True)
    return jnp.sum(parts, axis=0)


def contract_rows(left_side, right_side):
    return lax.dot_general(left_side, right_side, (((0,), (0,)), ((), ())), precision=precise)


def per_device(
    bands_in,
    cell_ham,
    cell_nodes,
    left_face,
    right_face,
    proj_values,
    proj_nodes,
    slot_owner,
    slot_atom,
    coupling,
    node_weight,
    filter_center,
    filter_half,
):
    columns = bands_in.shape[1]
    scalars = jnp.stack([filter_center[0], filter_half[0]]).reshape(1, 2)
    filtered = run_filter(
        scalars, bands_in, cell_ham, cell_nodes, left_face, right_face, proj_values, proj_nodes, slot_owner, slot_atom, coupling
    )
    weighted = filtered * node_weight[:, None]
    groups = lax.axis_size("band")
    reach_count = groups // 2
    blocks = [contract_rows(weighted, filtered)]
    for offset in range(1, reach_count + 1):
        partner = passed_along(filtered, "band", -offset)
        blocks.append(contract_rows(weighted, partner))
    mirrored = []
    for offset in range(1, groups - reach_count):
        mirrored.append(passed_along(blocks[offset].T, "band", offset))
    blocks = blocks + mirrored[::-1]
    row_block = jnp.roll(jnp.concatenate(blocks, axis=1), lax.axis_index("band") * columns, axis=1)
    margin = sum_at_owner(row_block, "mesh", 1)
    return (filtered, margin)


def solution(mesh):
    placed = (
        P("mesh", "band"),
        P("mesh", None, None),
        P("mesh", None),
        P("mesh", None),
        P("mesh", None),
        P("mesh", None, None),
        P("mesh", None),
        P("mesh", None),
        P("mesh"),
        P("mesh", None, None),
        P("mesh"),
        P(),
        P(),
    )
    return jax.shard_map(
        per_device,
        mesh=mesh,
        in_specs=placed,
        out_specs=(P("mesh", "band"), P("band", "mesh")),
        check_vma=False,
    )
```

time: 743 us -> 421 us (0.57); the launches traced: 733 us -> 420 us
  Pallas kernels: 0 us -> 209 us
  other arithmetic: 141 us -> 4.07 us
  local copies, waits for them, and re-layouts: 154 us -> 26.3 us
  blocking collectives: 151 us -> 60 us
  matrix products: 105 us -> 19 us
  starting transfers between devices: 108 us -> 54.4 us
  waiting for transfers between devices: 70.8 us -> 44.8 us
    pallas_call x0 -> x1, Pallas kernels: none -> 209 us  [run_filter(): pl.pallas_call(filter_kernel, out_shape=jax.ShapeDtypeStruct((NODES, COLS...]
    scatter-add x12 -> x0, other arithmetic: 126 us -> none  [the longest x3 71.5 us: nonlocal_term(): jnp.zeros_like(vectors).at[proj_nodes.reshape(-1)]]
    all_to_all x2 -> x0, blocking collectives: 88.4 us -> none  [nonlocal_term(): lax.all_to_all(outgoing, 'mesh', split_axis=0, concat_axis=0, tiled=True)]
    gather x12 -> x0, local copies, waits for them, and re-layouts: 85.4 us -> none  [the longest x3 51.9 us: nonlocal_term(): selected = vectors[proj_nodes]]
    dot_general x18 -> x0, matrix products: 73.2 us -> none  [the longest x3 23.1 us: cell_apply(): jnp.einsum('cij,cjb->cib', hamiltonians, gathered, precision=precise)]
    all_to_all x5 -> x0, starting transfers between devices: 37.1 us -> none  [the longest x3 16 us: nonlocal_term(): lax.all_to_all(returning, 'mesh', split_axis=0, concat_axis=0, tiled=True)]
    all_to_all x5 -> x0, waiting for transfers between devices: 32 us -> none  [the longest x1 32 us: nonlocal_term(): lax.all_to_all(outgoing, 'mesh', split_axis=0, concat_axis=0, tiled=True)]
    reshape x12 -> x2, local copies, waits for them, and re-layouts: 30 us -> 0.17 us  [the longest x1 0.1 us: run_filter(): source[:, 32:].reshape(-1)]
  transfers between devices with their start and end apart: 18 -> 7, of which waited for: 6 -> 4; matrix products, arithmetic and copies ran while one was open for 25% -> 6% of each run, Pallas kernels for 0% -> 0%
where the time goes in v1:
time: 421 us; the launch traced here: 420 us
  Pallas kernels  209 us (50%)
  blocking collectives  60 us (14%)
  starting transfers between devices  54.4 us (13%)
  waiting for transfers between devices  44.8 us (11%)
  local copies, waits for them, and re-layouts  26.3 us (6%)
  matrix products  19 us (5%)
    pallas_call x1, Pallas kernels, run_filter(): pl.pallas_call(filter_kernel, out_shape=jax.ShapeDtypeStruct((NODES, COLS...  209 us
    all_to_all x1, blocking collectives, sum_at_owner(): parts = lax.all_to_all(cut_along(array, dim, count), axis, 0, 0, tiled=True)  60 us
    ppermute x7, starting transfers between devices, passed_along(): return lax.ppermute(block, axis, route)  54.4 us
    ppermute x7, waiting for transfers between devices, passed_along(): return lax.ppermute(block, axis, route)  44.8 us
    dot_general x5, matrix products, contract_rows(): lax.dot_general(left_side, right_side, (((0,), (0,)), ((), ())), precisio...  19 us
    unnamed x22, local copies, waits for them, and re-layouts  16.7 us
  transfers between devices with their start and end apart: 7, of which 4 were waited for; matrix products, arithmetic and copies ran while one was open for 6% of the time, Pallas kernels for 0%

profile of v1, /device:TPU:48, one launch (start us, length us, event | category | flops | bytes accessed | tf_op | source)
XLA Modules:
  0.0 420.0 jit_solution(7383572426746830228)
XLA Ops:
  0.7 0.1 and_select_fusion
  0.7 0.1 broadcast_compare_fusion
  0.8 0.9 convert_reduce_fusion
  1.7 0.7 multiply_add_fusion
  2.4 0.7 broadcast_add_fusion.2
  3.1 0.1 select_reduce_fusion
  3.2 0.1 sub.15
  3.3 0.2 slice_reduce_fusion.3
  3.5 0.1 fusion.16
  3.5 0.1 slice.27
  3.6 0.1 reshape.138
  3.7 0.1 reshape.137
  3.8 1.1 broadcast_in_dim.128.row_source
  4.9 0.1 sub.17
  5.0 0.2 slice_reduce_fusion.1
  5.2 0.7 constant_dynamic-update-slice_fusion.1
  5.8 0.7 constant_dynamic-update-slice_fusion.face_row
  6.5 0.8 copy.34.face_col
  7.3 1.0 copy.40
  8.2 1.9 copy.35.proj_values
  10.1 1.6 copy.31
  11.7 1.4 copy.32
  14.4 0.7 pad.4.clone
  15.1 0.7 maximum_bitcast_fusion.scalars
  15.8 0.1 select_convert_fusion
  15.8 0.7 broadcast_in_dim.127.labels
  16.5 209.4 %filter_bands.1 = f32[1024,256]{1,0:T(8,128)} custom-call(f32[1,2]{1,0:T(1,128)} %maximum_bitcast_fusion.scalars, f32[1024,256]{1,0:T(8,128)} %bands_in.1, f32[3,512,512]{2,1,0:T(8,128)} %cell_ham.1, s32[3,512]{1,0:T(4,128)} %cell_rows.1, s32[512,3]{1,0:T(8,128)} %bitcast.21, s32[1,256]{1,0:T(1,128)} %copy-done.2, s32[256,1]{1,0:T(8,128)} %copy.34.face_col, ...), custom_call_target="tpu_custom_call" | custom-call | tf_op jit(solution)/shard_map/filter_bands/pallas_call | solution.py:409
  225.9 0.1 collective-permute-start
  226.0 1.2 collective-permute-start.1
  227.2 3.6 collective-permute-start.2
  230.8 1.3 collective-permute-start.3
  232.1 4.2 %constant_dynamic-update-slice_fusion.17 = (f32[256,4096]{0,1:T(8,128)}, f32[256,256]{0,1:T(8,128)S(1)}) fusion(f32[1024,256]{1,0:T(8,128)} %filter_bands.1, f32[1024]{0:T(1024)S(1)} %copy-done.1), kind=kOutput, calls=%fused_computation.32 | convolution fusion | flops 805568512 | bytes 2625536 | tf_op jit(solution)/shard_map/dot_general | solution.py:495
  236.3 16.0 %collective-permute-done = f32[1024,256]{1,0:T(8,128)} collective-permute-done((f32[1024,256]{1,0:T(8,128)}, f32[1024,256]{1,0:T(8,128)}, u32[]{:S(2)}, u32[]{:S(2)}) %collective-permute-start) | collective-permute-done | bytes 1048608 | tf_op jit(solution)/shard_map/ppermute | solution.py:479
  252.4 4.2 %constant_dynamic-update-slice_fusion.16 = (f32[256,4096]{0,1:T(8,128)}, f32[256,256]{0,1:T(8,128)S(1)}) fusion(f32[256,4096]{0,1:T(8,128)} %get-tuple-element.8, f32[1024,256]{1,0:T(8,128)} %collective-permute-done, f32[1024,256]{1,0:T(8,128)} %filter_bands.1, f32[1024]{0:T(1024)S(1)} %copy-done.1), kind=kOutput, calls=%fused_computation.31 | convolution fusion | flops 805568512 | bytes 2625536 | tf_op jit(solution)/shard_map/dot_general | solution.py:495
  256.6 18.3 %collective-permute-done.1 = f32[1024,256]{1,0:T(8,128)} collective-permute-done((f32[1024,256]{1,0:T(8,128)}, f32[1024,256]{1,0:T(8,128)}, u32[]{:S(2)}, u32[]{:S(2)}) %collective-permute-start.1) | collective-permute-done | bytes 1048608 | tf_op jit(solution)/shard_map/ppermute | solution.py:479
  274.9 3.9 constant_dynamic-update-slice_fusion.15
  278.8 0.0 collective-permute-done.2
  278.8 3.9 constant_dynamic-update-slice_fusion.14
  282.7 0.8 copy.37
  283.5 47.7 %collective-permute-start.4 = (f32[256,256]{0,1:T(8,128)}, f32[256,256]{0,1:T(8,128)S(1)}, u32[]{:S(2)}, u32[]{:S(2)}) collective-permute-start(f32[256,256]{0,1:T(8,128)} %bitcast.24), channel_id=1, source_target_pairs={{160,0},{192,32},{224,64},{0,96},{32,128},{64,160},{96,192},{128,2... | collective-permute-start | bytes 786440 | tf_op jit(solution)/shard_map/ppermute | solution.py:479
  331.2 0.8 copy.38
  332.1 0.0 collective-permute-start.5
  332.1 0.9 copy.39
  332.9 0.6 collective-permute-start.6
  333.5 0.0 collective-permute-done.3
  333.5 2.7 constant_dynamic-update-slice_fusion.13
  336.2 2.0 collective-permute-done.4
  338.2 0.7 constant_dynamic-update-slice_fusion.12
  339.0 8.4 %collective-permute-done.5 = f32[256,256]{0,1:T(8,128)} collective-permute-done((f32[256,256]{0,1:T(8,128)}, f32[256,256]{0,1:T(8,128)}, u32[]{:S(2)}, u32[]{:S(2)}) %collective-permute-start.5) | collective-permute-done | bytes 262176 | tf_op jit(solution)/shard_map/ppermute | solution.py:479
  347.4 1.7 constant_dynamic-update-slice_fusion.11
  349.0 0.0 collective-permute-done.6
  349.0 0.7 constant_dynamic-update-slice_fusion.10
  349.8 0.7 constant_dynamic-update-slice_fusion.9
  350.5 0.7 constant_dynamic-update-slice_fusion.8
  351.2 0.7 constant_dynamic-update-slice_fusion.7
  351.9 0.7 constant_dynamic-update-slice_fusion.6
  352.7 0.7 constant_dynamic-update-slice_fusion.5
  353.4 0.7 constant_dynamic-update-slice_fusion.4
  354.1 1.7 constant_dynamic-update-slice_fusion.3
  355.8 0.7 constant_dynamic-update-slice_fusion.2
  356.5 1.7 constant_dynamic-slice_fusion
  358.3 60.0 %all_to_all.5 = f32[32,256,64]{1,2,0:T(8,128)S(1)} all-to-all(f32[32,256,64]{1,2,0:T(8,128)S(1)} %bitcast.20), channel_id=1, replica_groups=mesh['band'=8,'mesh'=32] {'mesh'}, dimensions={0} | all-to-all | bytes 4194304 | tf_op jit(solution)/shard_map/all_to_all | solution.py:490
  418.3 0.8 reduce_sum.39
  419.1 1.0 copy.60
  (12 shorter events, 0.0 us)
Async XLA Ops:
  6.5 10.0 %copy-start.2 = (s32[1,256]{1,0:T(1,128)}, s32[1,256]{1,0:T(1,128)S(1)}, u32[]{:S(2)}) copy-start(s32[1,256]{1,0:T(1,128)S(1)} %constant_dynamic-update-slice_fusion.face_row) | copy-start | bytes 3076
  10.1 222.0 %copy-start.1 = (f32[1024]{0:T(1024)S(1)}, f32[1024]{0:T(1024)}, u32[]{:S(2)}) copy-start(f32[1024]{0:T(1024)} %param.23) | copy-start | bytes 12292
  225.9 48.9 %copy-start = (f32[1024,256]{1,0:T(8,128)S(1)}, f32[1024,256]{1,0:T(8,128)}, u32[]{:S(2)}) copy-start(f32[1024,256]{1,0:T(8,128)} %filter_bands.1) | copy-start | bytes 3145732
  225.9 26.4 %collective-permute-start = (f32[1024,256]{1,0:T(8,128)}, f32[1024,256]{1,0:T(8,128)}, u32[]{:S(2)}, u32[]{:S(2)}) collective-permute-start(f32[1024,256]{1,0:T(8,128)} %filter_bands.1), channel_id=1, source_target_pairs={{32,0},{64,32},{96,64},{128,96},{160,128},{192,160},{224,192},{0,2... | collective-permute-start | bytes 3145736 | tf_op jit(solution)/shard_map/ppermute | solution.py:479
  226.0 48.8 %collective-permute-start.1 = (f32[1024,256]{1,0:T(8,128)}, f32[1024,256]{1,0:T(8,128)}, u32[]{:S(2)}, u32[]{:S(2)}) collective-permute-start(f32[1024,256]{1,0:T(8,128)} %filter_bands.1), channel_id=1, source_target_pairs={{64,0},{96,32},{128,64},{160,96},{192,128},{224,160},{0,192},{32,2... | collective-permute-start | bytes 3145736 | tf_op jit(solution)/shard_map/ppermute | solution.py:479
  227.2 51.6 %collective-permute-start.2 = (f32[1024,256]{1,0:T(8,128)}, f32[1024,256]{1,0:T(8,128)}, u32[]{:S(2)}, u32[]{:S(2)}) collective-permute-start(f32[1024,256]{1,0:T(8,128)} %filter_bands.1), channel_id=1, source_target_pairs={{96,0},{128,32},{160,64},{192,96},{224,128},{0,160},{32,192},{64,2... | collective-permute-start | bytes 3145736 | tf_op jit(solution)/shard_map/ppermute | solution.py:479
  230.8 102.6 %collective-permute-start.3 = (f32[1024,256]{1,0:T(8,128)}, f32[1024,256]{1,0:T(8,128)S(1)}, u32[]{:S(2)}, u32[]{:S(2)}) collective-permute-start(f32[1024,256]{1,0:T(8,128)} %filter_bands.1), channel_id=1, source_target_pairs={{128,0},{160,32},{192,64},{224,96},{0,128},{32,160},{64,192},{96,2... | collective-permute-start | bytes 3145736 | tf_op jit(solution)/shard_map/ppermute | solution.py:479
  283.5 54.7 %collective-permute-start.4 = (f32[256,256]{0,1:T(8,128)}, f32[256,256]{0,1:T(8,128)S(1)}, u32[]{:S(2)}, u32[]{:S(2)}) collective-permute-start(f32[256,256]{0,1:T(8,128)} %bitcast.24), channel_id=1, source_target_pairs={{160,0},{192,32},{224,64},{0,96},{32,128},{64,160},{96,192},{128,2... | collective-permute-start | bytes 786440 | tf_op jit(solution)/shard_map/ppermute | solution.py:479
  332.1 15.3 %collective-permute-start.5 = (f32[256,256]{0,1:T(8,128)}, f32[256,256]{0,1:T(8,128)}, u32[]{:S(2)}, u32[]{:S(2)}) collective-permute-start(f32[256,256]{0,1:T(8,128)} %bitcast.25), channel_id=1, source_target_pairs={{192,0},{224,32},{0,64},{32,96},{64,128},{96,160},{128,192},{160,2... | collective-permute-start | bytes 786440 | tf_op jit(solution)/shard_map/ppermute | solution.py:479
  332.9 16.1 %collective-permute-start.6 = (f32[256,256]{0,1:T(8,128)}, f32[256,256]{0,1:T(8,128)S(1)}, u32[]{:S(2)}, u32[]{:S(2)}) collective-permute-start(f32[256,256]{0,1:T(8,128)} %bitcast.26), channel_id=1, source_target_pairs={{224,0},{0,32},{32,64},{64,96},{96,128},{128,160},{160,192},{192,2... | collective-permute-start | bytes 786440 | tf_op jit(solution)/shard_map/ppermute | solution.py:479

commit v2 on v1

--- a/solution.py
+++ b/solution.py
@@ -1,5 +1,3 @@
-import functools
-
 import jax
 import jax.numpy as jnp
 from jax import lax
@@ -8,7 +6,6 @@
 from jax.sharding import PartitionSpec as P
 
 MESH = pl.DeviceIdType.MESH
-precise = lax.Precision.HIGHEST
 f32, bf16, i32 = jnp.float32, jnp.bfloat16, jnp.int32
 
 PARTS = 32
@@ -25,6 +22,7 @@
 ROWS = MAIN + PARTS * 8
 TERMS = ATOMS * PADDED
 BLOCK = 256
+GROUPS = 8
 
 
 def mm(a, b):
@@ -69,7 +67,9 @@
     row_source,
     labels,
     coupling,
+    node_weight,
     filtered,
+    margin,
     b24,
     b24h,
     b24l,
@@ -110,9 +110,28 @@
     rl,
     sf,
     rf,
+    wth,
+    wtl,
+    halves,
+    kept,
+    given,
+    core_in,
+    strips,
+    turned,
+    swapped,
+    sh,
+    rh,
+    sc,
+    rc,
+    ss,
+    rs,
+    sw,
+    rw,
 ):
     me = lax.axis_index("mesh")
     band = lax.axis_index("band")
+    other = me // 4
+    quarter = lax.rem(me, 4)
     centre, half = scalars[0, 0], scalars[0, 1]
 
     def peer(k):
@@ -125,6 +144,19 @@
         pl.semaphore_signal(barrier, inc=1, device_id=(band, peer(k + 1)), device_id_type=MESH)
 
     loop(PARTS - 1, greet)
+
+    def greet_group(k):
+        group = lax.rem(band + k + 1, GROUPS)
+        pl.semaphore_signal(barrier, inc=1, device_id=(group, me), device_id_type=MESH)
+
+    loop(GROUPS - 1, greet_group)
+
+    @pl.when(other != band)
+    def _():
+        def greet_mirror(j):
+            pl.semaphore_signal(barrier, inc=1, device_id=(other, band * 4 + j), device_id_type=MESH)
+
+        loop(4, greet_mirror)
 
     b24[...] = jnp.zeros_like(b24)
     for s in range(SLOTS):
@@ -223,7 +255,7 @@
         at = rows_at(i)
         return mm(b8h[at, :], vh[...]) + (mm(b8h[at, :], vl[...]) + mm(b8l[at, :], vh[...]))
 
-    pl.semaphore_wait(barrier, PARTS - 1)
+    pl.semaphore_wait(barrier, jnp.where(other != band, 4, 0) + PARTS - 1 + GROUPS - 1)
 
     def tell(k):
         copy_to(labels, lab_in, sl, rl, peer(k + 1)).start()
@@ -383,9 +415,144 @@
             exchange(coefficient, out1, in1, s1, r1)
 
     loop(3, degree)
-
-
-def run_filter(scalars, bands_in, cell_ham, cell_nodes, left_face, right_face, proj_values, proj_nodes, slot_owner, slot_atom, coupling):
+    margin_of(
+        me, band, other, quarter, node_weight, filtered, margin, vh, vl, wth, wtl, halves, kept, given, core_in, strips,
+        turned, swapped, sh, rh, sc, rc, ss, rs, sw, rw,
+    )
+
+
+def margin_of(
+    me, band, other, quarter, node_weight, filtered, margin, vh, vl, wth, wtl, halves, kept, given, core_in, strips,
+    turned, swapped, sh, rh, sc, rc, ss, rs, sw, rw,
+):
+    y, x = band // 2, lax.rem(band, 2)
+    core, chip = lax.rem(me, 2), me // 2
+    sibling = me + 1 - 2 * core
+    steps = (
+        (0, 1, x, 1 - x),
+        (1, 0, 0, 0),
+        (3, 0, 1, 1),
+        (1, 1, 0, 0),
+        (3, 1, 1, 1),
+        (2, 0, y // 2, 1 - y // 2),
+        (2, 1, y // 2, 1 - y // 2),
+    )
+
+    def group_at(dy, dx):
+        return lax.rem(y + dy, 4) * 2 + lax.rem(x + dx, 2)
+
+    def half_copy(i):
+        dy, dx, mine, _ = steps[i]
+        return pltpu.make_async_remote_copy(
+            filtered.at[rows_at(mine, NODES // 2)],
+            halves.at[i],
+            sh.at[i],
+            rh.at[i],
+            device_id=(group_at(dy, dx), me),
+            device_id_type=MESH,
+        )
+
+    def core_copy(i):
+        return pltpu.make_async_remote_copy(
+            given.at[i], core_in.at[i], sc.at[i], rc.at[i], device_id=(band, sibling), device_id_type=MESH
+        )
+
+    def strip_copy(i, j, target):
+        return pltpu.make_async_remote_copy(
+            kept.at[i, j], strips.at[chip], ss.at[i, j], rs.at[chip], device_id=(band, target), device_id_type=MESH
+        )
+
+    for i in range(7):
+        half_copy(i).start()
+    for i in range(NODES // BLOCK):
+        at = slice(i * BLOCK, (i + 1) * BLOCK)
+        high, low = split(filtered[at, :].T * node_weight[:, at])
+        wth[:, at] = high
+        wtl[:, at] = low
+    lower = iota((128, 128), 1) < 64
+    owners = [band] + [group_at((4 - dy) % 4, dx) for dy, dx, _, _ in steps]
+
+    def send_strips(i):
+        core_copy(i).wait_recv()
+        for j in range(2):
+            kept[i, j] = kept[i, j] + core_in[i, j]
+            target = owners[i] * 4 + 2 * j + core
+
+            @pl.when(target == me)
+            def _():
+                strips[chip] = kept[i, j]
+
+            @pl.when(target != me)
+            def _():
+                strip_copy(i, j, target).start()
+
+    for i in range(GROUPS):
+        if i == 0:
+            product = mm(wth[...], vh[...]) + (mm(wth[...], vl[...]) + mm(wtl[...], vh[...]))
+        else:
+            half_copy(i - 1).wait_recv()
+            at = rows_at(steps[i - 1][3], NODES // 2)
+            high, low = split(halves[i - 1])
+            product = mm(wth[:, at], high) + (mm(wth[:, at], low) + mm(wtl[:, at], high))
+        for j in range(2):
+            top, bottom = product[:128, j * 128 : (j + 1) * 128], product[128:, j * 128 : (j + 1) * 128]
+            even = jnp.where(lower, top, pltpu.roll(bottom, 64, 1))
+            odd = jnp.where(lower, pltpu.roll(top, 64, 1), bottom)
+            kept[i, j] = jnp.where(core == 0, even, odd)
+            given[i, j] = jnp.where(core == 0, odd, even)
+        core_copy(i).start()
+        if i > 0:
+            send_strips(i - 1)
+    send_strips(GROUPS - 1)
+
+    def arrived(k):
+        source = lax.rem(chip + k + 1, PARTS // 2)
+        pltpu.make_async_remote_copy(
+            kept.at[0, 0], strips.at[source], ss.at[0, 0], rs.at[source], device_id=(band, source * 2 + core), device_id_type=MESH
+        ).wait_recv()
+
+    loop(PARTS // 2 - 1, arrived)
+    total = jnp.sum(strips[...], axis=0)
+    margin[0:128, :] = total[:, :64]
+    margin[128:256, :] = total[:, 64:]
+
+    def swap_copy(j):
+        return pltpu.make_async_remote_copy(
+            turned.at[pl.ds(64 * (j // 2), 64)],
+            swapped.at[quarter],
+            sw.at[j],
+            rw.at[quarter],
+            device_id=(other, band * 4 + j),
+            device_id_type=MESH,
+        )
+
+    @pl.when(other != band)
+    def _():
+        turned[...] = total.T
+        for j in range(4):
+            swap_copy(j).start()
+        for j in range(4):
+            pltpu.make_async_remote_copy(
+                turned.at[pl.ds(0, 64)], swapped.at[j], sw.at[j], rw.at[j], device_id=(other, band * 4 + j), device_id_type=MESH
+            ).wait_recv()
+            tile = jnp.where(lax.rem(quarter, 2) == 0, swapped[j][:, :64], swapped[j][:, 64:])
+            margin[j * 64 : (j + 1) * 64, :] += tile
+        for j in range(4):
+            swap_copy(j).wait_send()
+
+    for i in range(7):
+        half_copy(i).wait_send()
+    for i in range(GROUPS):
+        core_copy(i).wait_send()
+        for j in range(2):
+            target = owners[i] * 4 + 2 * j + core
+
+            @pl.when(target != me)
+            def _():
+                strip_copy(i, j, target).wait_send()
+
+
+def run_filter(scalars, bands_in, cell_ham, cell_nodes, left_face, right_face, proj_values, proj_nodes, slot_owner, slot_atom, coupling, node_weight):
     owners = slot_owner[:, 0]
     ordinal = jnp.arange(SLOTS)
     position = jnp.sum((owners[:, None] == owners[None, :]) & (ordinal[None, :] < ordinal[:, None]), axis=1)
@@ -408,9 +575,9 @@
     V = pltpu.VMEM
     return pl.pallas_call(
         filter_kernel,
-        out_shape=jax.ShapeDtypeStruct((NODES, COLS), f32),
-        in_specs=[pl.BlockSpec(memory_space=pltpu.SMEM)] + [vmem] * 11,
-        out_specs=vmem,
+        out_shape=(jax.ShapeDtypeStruct((NODES, COLS), f32), jax.ShapeDtypeStruct((COLS, 64), f32)),
+        in_specs=[pl.BlockSpec(memory_space=pltpu.SMEM)] + [vmem] * 12,
+        out_specs=(vmem, vmem),
         scratch_shapes=[
             V((SLOTS * PADDED, NODES), f32),
             V((SLOTS * PADDED, NODES), bf16),
@@ -452,6 +619,23 @@
             D((PARTS,)),
             D((2,)),
             D((3, 2)),
+            V((COLS, NODES), bf16),
+            V((COLS, NODES), bf16),
+            V((7, NODES // 2, COLS), f32),
+            V((GROUPS, 2, 128, 128), f32),
+            V((GROUPS, 2, 128, 128), f32),
+            V((GROUPS, 2, 128, 128), f32),
+            V((PARTS // 2, 128, 128), f32),
+            V((128, 128), f32),
+            V((4, 64, 128), f32),
+            D((7,)),
+            D((7,)),
+            D((GROUPS,)),
+            D((GROUPS,)),
+            D((GROUPS, 2)),
+            D((PARTS // 2,)),
+            D((4,)),
+            D((4,)),
         ],
         compiler_params=pltpu.CompilerParams(
             collective_id=0, has_side_effects=True, vmem_limit_bytes=58 * 2**20
@@ -470,29 +654,8 @@
         row_source.astype(i32),
         labels,
         padded,
+        node_weight[None, :],
     )
-
-
-def passed_along(block, axis, distance):
-    devices = range(lax.axis_size(axis))
-    route = [((i - distance) % len(devices), i) for i in devices]
-    return lax.ppermute(block, axis, route)
-
-
-def cut_along(array, dim, count):
-    lengths = array.shape
-    parts = array.reshape(*lengths[:dim], count, lengths[dim] // count, *lengths[dim + 1 :])
-    return jnp.moveaxis(parts, dim, 0)
-
-
-def sum_at_owner(array, axis, dim):
-    count = lax.axis_size(axis)
-    parts = lax.all_to_all(cut_along(array, dim, count), axis, 0, 0, tiled=True)
-    return jnp.sum(parts, axis=0)
-
-
-def contract_rows(left_side, right_side):
-    return lax.dot_general(left_side, right_side, (((0,), (0,)), ((), ())), precision=precise)
 
 
 def per_device(
@@ -510,25 +673,11 @@
     filter_center,
     filter_half,
 ):
-    columns = bands_in.shape[1]
     scalars = jnp.stack([filter_center[0], filter_half[0]]).reshape(1, 2)
-    filtered = run_filter(
-        scalars, bands_in, cell_ham, cell_nodes, left_face, right_face, proj_values, proj_nodes, slot_owner, slot_atom, coupling
+    return run_filter(
+        scalars, bands_in, cell_ham, cell_nodes, left_face, right_face, proj_values, proj_nodes, slot_owner, slot_atom, coupling,
+        node_weight,
     )
-    weighted = filtered * node_weight[:, None]
-    groups = lax.axis_size("band")
-    reach_count = groups // 2
-    blocks = [contract_rows(weighted, filtered)]
-    for offset in range(1, reach_count + 1):
-        partner = passed_along(filtered, "band", -offset)
-        blocks.append(contract_rows(weighted, partner))
-    mirrored = []
-    for offset in range(1, groups - reach_count):
-        mirrored.append(passed_along(blocks[offset].T, "band", offset))
-    blocks = blocks + mirrored[::-1]
-    row_block = jnp.roll(jnp.concatenate(blocks, axis=1), lax.axis_index("band") * columns, axis=1)
-    margin = sum_at_owner(row_block, "mesh", 1)
-    return (filtered, margin)
 
 
 def solution(mesh):

time: 421 us -> 322 us (0.76)
  the two profiles are of different devices: /device:TPU:48 before, /device:TPU:249 now
where the time goes in v2:
time: 322 us; the launch traced here: 319 us
  Pallas kernels  298 us (93%)
  local copies, waits for them, and re-layouts  15.1 us (5%)
  other arithmetic  3.22 us (1%)
    pallas_call x1, Pallas kernels, run_filter(): pl.pallas_call(filter_kernel, out_shape=(jax.ShapeDtypeStruct((NODES, COL...  298 us
    unnamed x8, local copies, waits for them, and re-layouts  8.75 us

profile of v2, /device:TPU:249, one launch (start us, length us, event | category | flops | bytes accessed | tf_op | source)
XLA Modules:
  0.0 318.6 jit_solution(1896540555834281782)
XLA Ops:
  1.9 0.6 maximum_bitcast_fusion.scalars
  2.5 0.1 and_select_fusion
  2.6 0.1 broadcast_compare_fusion
  2.7 0.7 broadcast_add_fusion.2
  3.3 0.9 convert_reduce_fusion
  4.2 0.7 multiply_add_fusion
  4.9 0.1 select_reduce_fusion
  5.0 0.7 constant_dynamic-update-slice_fusion.1
  5.7 0.7 constant_dynamic-update-slice_fusion.face_row
  6.3 0.0 copy-start
  6.3 0.1 sub.13
  6.4 0.2 slice_reduce_fusion.1
  6.6 0.1 select_convert_fusion
  6.7 0.1 sub.11
  6.8 0.2 slice_reduce_fusion.3
  7.0 0.1 fusion.1
  7.1 0.1 reshape.133
  7.1 0.1 slice.27
  7.2 0.1 reshape.134
  7.3 1.4 copy.28
  8.8 0.7 broadcast_in_dim.129.labels
  9.4 0.8 copy.30.face_col
  10.2 1.0 copy.34
  11.2 0.7 pad.4.clone
  11.9 1.5 copy.27
  13.4 1.9 copy.31.proj_values
  15.3 1.1 broadcast_in_dim.131.row_source
  16.4 0.0 copy-done
  16.4 298.3 %filter_bands.1 = (f32[1024,256]{1,0:T(8,128)}, f32[256,64]{1,0:T(8,128)}) custom-call(f32[1,2]{1,0:T(1,128)} %maximum_bitcast_fusion.scalars, f32[1024,256]{1,0:T(8,128)} %bands_in.1, f32[3,512,512]{2,1,0:T(8,128)} %cell_ham.1, s32[3,512]{1,0:T(4,128)} %cell_rows.1, s32[512,3]{1,0:T(8,128)} %bitcast.10, s32[1,256]{1,0:T(1,128)} %copy-done, ...), custom_call_target="tpu_custom_call" | custom-call | tf_op jit(solution)/shard_map/filter_bands/pallas_call | solution.py:576
  314.7 1.6 copy.33
  316.3 2.3 copy.39
  (6 shorter events, 0.0 us)
Async XLA Ops:
  6.3 10.1 %copy-start = (s32[1,256]{1,0:T(1,128)}, s32[1,256]{1,0:T(1,128)S(1)}, u32[]{:S(2)}) copy-start(s32[1,256]{1,0:T(1,128)S(1)} %constant_dynamic-update-slice_fusion.face_row) | copy-start | bytes 3076

commit v3 on v2

v3 whole, which is shorter than its diff:
```python
import jax
import jax.numpy as jnp
from jax import lax
from jax.experimental import pallas as pl
from jax.experimental.pallas import tpu as pltpu
from jax.sharding import PartitionSpec as P

MESH = pl.DeviceIdType.MESH
f32, bf16, i32 = jnp.float32, jnp.bfloat16, jnp.int32

PARTS = 32
NODES = 1024
COLS = 256
SLOTS = 32
PROJ = 18
PADDED = 24
ATOMS = 16
CELLS = 3
CELL = 512
FACE = 128
WIDE = 40
ROWS = PARTS * WIDE
TERMS = ATOMS * PADDED
BLOCK = 256
GROUPS = 8


def mm(a, b):
    return jnp.dot(a, b, preferred_element_type=f32)


def split(x):
    high = x.astype(bf16)
    return high, (x - high.astype(f32)).astype(bf16)


def iota(shape, dim):
    return lax.broadcasted_iota(i32, shape, dim)


def hot(mask):
    return jnp.where(mask, 1.0, 0.0).astype(bf16)


def rows_at(index, size=BLOCK):
    return pl.ds(pl.multiple_of(index * size, size), size)


def loop(count, body):
    def step(i, carry):
        body(i)
        return carry

    lax.fori_loop(0, count, step, 0)


def filter_kernel(
    centre_ref,
    half_ref,
    bands_in,
    cell_ham,
    cell_nodes,
    left_face,
    right_face,
    proj_values,
    proj_nodes,
    slot_owner,
    slot_atom,
    coupling,
    node_weight,
    filtered,
    margin,
    stacked,
    coupled,
    b24,
    b24h,
    b24l,
    b24th,
    b24tl,
    place,
    placet,
    gat,
    sca,
    fgat,
    fsca,
    member,
    memt,
    cbh,
    cbl,
    vh,
    vl,
    xh,
    xl,
    gh,
    gl,
    ph,
    plo,
    cells,
    previous,
    out1,
    in1,
    out2,
    in2,
    labels,
    lab_in,
    face_out,
    face_in,
    s1,
    r1,
    s2,
    r2,
    sl,
    rl,
    sf,
    rf,
    wth,
    wtl,
    halves,
    kept,
    given,
    core_in,
    strips,
    turned,
    swapped,
    sh,
    rh,
    sc,
    rc,
    ss,
    rs,
    sw,
    rw,
):
    me = lax.axis_index("mesh")
    band = lax.axis_index("band")
    other = me // 4
    quarter = lax.rem(me, 4)
    centre, half = centre_ref[0], half_ref[0]

    def peer(k):
        return lax.rem(me + k, PARTS)

    face_in[...] = jnp.zeros_like(face_in)
    in1[...] = jnp.zeros_like(in1)
    in2[...] = jnp.zeros_like(in2)
    barrier = pltpu.get_barrier_semaphore()

    def greet(k):
        pl.semaphore_signal(barrier, inc=1, device_id=(band, peer(k + 1)), device_id_type=MESH)

    loop(PARTS - 1, greet)

    def greet_group(k):
        group = lax.rem(band + k + 1, GROUPS)
        pl.semaphore_signal(barrier, inc=1, device_id=(group, me), device_id_type=MESH)

    loop(GROUPS - 1, greet_group)

    @pl.when(other != band)
    def _():
        def greet_mirror(j):
            pl.semaphore_signal(barrier, inc=1, device_id=(other, band * 4 + j), device_id_type=MESH)

        loop(4, greet_mirror)

    stacked[...] = jnp.zeros_like(stacked)
    for s in range(SLOTS):
        stacked[s * PADDED : s * PADDED + PROJ, :] = proj_values[:, s, :]
    slot_cols = proj_nodes[...].astype(f32).T
    node = iota((128, NODES), 1).astype(f32)
    upper = lax.rem(iota((4 * PADDED, 128), 0), 2 * PADDED) < PADDED
    for t in range(SLOTS // 2):
        at = slice(t * 2 * PADDED, (t + 1) * 2 * PADDED)
        spread = jnp.concatenate([hot(slot_cols[:, s : s + 1] == node) for s in (2 * t, 2 * t + 1)], axis=0)
        values = stacked[at, :]
        high = values.astype(bf16).astype(f32)
        both = jnp.concatenate([high, values - high], axis=0)
        both = jnp.concatenate([jnp.where(upper, both, 0.0), jnp.where(upper, 0.0, both)], axis=1)
        result = mm(both.astype(bf16), spread)
        b24[at, :] = result[: 2 * PADDED] + result[2 * PADDED :]
    high, low = split(b24[...])
    b24h[...] = high
    b24l[...] = low

    owner_row = slot_owner[...].astype(f32)
    atom_row = slot_atom[...].astype(f32)
    down, across = iota((SLOTS, SLOTS), 0), iota((SLOTS, SLOTS), 1)
    owner_col = jnp.sum(jnp.where(down == across, owner_row, 0.0), axis=1, keepdims=True)
    earlier = jnp.where((owner_col == owner_row) & (across < down), 1.0, 0.0)
    bucket_col = 2.0 * owner_col + jnp.sum(earlier, axis=1, keepdims=True)
    bucket_row = jnp.sum(jnp.where(down == across, bucket_col, 0.0), axis=0, keepdims=True)
    shape = (SLOTS, SLOTS * PADDED)
    spot = jnp.sum(jnp.where(iota(shape, 0) == iota(shape, 1) // PADDED, bucket_col, 0.0), axis=0, keepdims=True)
    lane = lax.rem(iota((1, SLOTS * PADDED), 1), PADDED)
    spot = jnp.where(lane < PROJ, spot.astype(i32) * PADDED + lane, -2)
    shape = (SLOTS * PADDED, SLOTS)
    spot_col = jnp.sum(jnp.where(iota(shape, 1) == iota(shape, 0) // PADDED, bucket_row, 0.0), axis=1, keepdims=True)
    lane = lax.rem(iota((SLOTS * PADDED, 1), 0), PADDED)
    spot_col = jnp.where(lane < PROJ, spot_col.astype(i32) * PADDED + lane, -2)

    def row_key(row):
        number = lax.rem(row, WIDE)
        key = (2 * (row // WIDE) + number // PROJ) * PADDED + lax.rem(number, PROJ)
        return jnp.where(number < 2 * PROJ, key, -1)

    for i in range(ROWS // BLOCK):
        at = slice(i * BLOCK, (i + 1) * BLOCK)
        place[at, :] = hot(row_key(iota((BLOCK, 1), 0) + i * BLOCK) == spot)

    previous[...] = bands_in[...]
    filtered[...] = bands_in[...]
    high, low = split(bands_in[...])
    vh[...] = high
    vl[...] = low

    def sides(h):
        return slice(h * 128, (h + 1) * 128)

    def copy_to(source, target, send, receive, h, o):
        return pltpu.make_async_remote_copy(
            source.at[h, o, pl.ds(0, 2 * PROJ)],
            target.at[h, me, pl.ds(0, 2 * PROJ)],
            send.at[h, o],
            receive.at[h, me],
            device_id=(band, o),
            device_id_type=MESH,
        )

    def arrival(source, target, send, receive, h, q):
        return pltpu.make_async_remote_copy(
            source.at[h, q, pl.ds(0, 2 * PROJ)],
            target.at[h, q, pl.ds(0, 2 * PROJ)],
            send.at[h, q],
            receive.at[h, q],
            device_id=(band, q),
            device_id_type=MESH,
        )

    def exchange(h, rows_of, out, target, send, receive):
        def group(t):
            g = lax.rem(me // 16 + 1 + t, 2)
            out[h, pl.ds(g * 16, 16)] = rows_of(rows_at(g, ROWS // 2)).reshape(16, WIDE, 128)

            def one(i):
                o = g * 16 + lax.rem(me + i, 16)

                @pl.when(o != me)
                def _():
                    copy_to(out, target, send, receive, h, o).start()

            loop(16, one)

        loop(2, group)
        target[h, me] = out[h, me]

    def collect(h, out, target, send, receive):
        def one(k):
            arrival(out, target, send, receive, h, peer(k + 1)).wait_recv()

        loop(PARTS - 1, one)
        high, low = split(target[h].reshape(ROWS, 128))
        xh[...] = high
        xl[...] = low

    def sent(h, out, target, send, receive):
        def one(k):
            arrival(out, target, send, receive, h, peer(k + 1)).wait_send()

        loop(PARTS - 1, one)

    def send_coefficients(h):
        columns = sides(h)
        fh, fl = vh[:, columns], vl[:, columns]
        high, low = split(mm(b24h[...], fh) + (mm(b24h[...], fl) + mm(b24l[...], fh)))
        exchange(h, lambda at: mm(place[at, :], high) + mm(place[at, :], low), out1, in1, s1, r1)

    pl.semaphore_wait(barrier, jnp.where(other != band, 4, 0) + PARTS - 1 + GROUPS - 1)
    for h in range(2):
        send_coefficients(h)

    target = iota((PARTS, SLOTS), 0).astype(f32) * 2.0
    first = jnp.sum(jnp.where(bucket_row == target, atom_row + 1.0, 0.0), axis=1, keepdims=True) - 1.0
    second = jnp.sum(jnp.where(bucket_row == target + 1.0, atom_row + 1.0, 0.0), axis=1, keepdims=True) - 1.0
    lane = iota((PARTS, 128), 1)
    named = jnp.where(lane < PROJ, first, jnp.where(lane < 2 * PROJ, second, -1.0))
    for o in range(PARTS):
        labels[o] = jnp.broadcast_to(named[o : o + 1, :], (8, 128))

    def label_to(o):
        return pltpu.make_async_remote_copy(
            labels.at[o], lab_in.at[me], sl.at[o], rl.at[me], device_id=(band, o), device_id_type=MESH
        )

    def label_from(q):
        return pltpu.make_async_remote_copy(
            labels.at[q], lab_in.at[q], sl.at[q], rl.at[q], device_id=(band, q), device_id_type=MESH
        )

    def tell(k):
        label_to(peer(k + 1)).start()

    loop(PARTS - 1, tell)
    lab_in[me] = labels[me]

    for i in range(NODES // BLOCK):
        at = slice(i * BLOCK, (i + 1) * BLOCK)
        row = iota((BLOCK, CELL), 0) + i * BLOCK
        for c in range(CELLS):
            mask = jnp.where(row == cell_nodes[c : c + 1, :], 1.0, 0.0)
            sca[at, c * CELL : (c + 1) * CELL] = mask.astype(bf16)
            gat[c * CELL : (c + 1) * CELL, at] = mask.T.astype(bf16)
        for side, face in enumerate((left_face, right_face)):
            mask = jnp.where(row[:, :FACE] == face[...], 1.0, 0.0)
            fsca[at, side * FACE : (side + 1) * FACE] = mask.astype(bf16)
            fgat[side * FACE : (side + 1) * FACE, at] = mask.T.astype(bf16)
    for i in range(SLOTS * PADDED // BLOCK):
        at = slice(i * BLOCK, (i + 1) * BLOCK)
        high, low = split(b24[at, :].T)
        b24th[:, at] = high
        b24tl[:, at] = low
        placet[at, :] = hot(spot_col[at, :] == row_key(iota((1, ROWS), 1)))
    coupled[...] = jnp.zeros_like(coupled)
    for a in range(ATOMS):
        coupled[a * PADDED : a * PADDED + PROJ, 0:PROJ] = coupling[:, a, :]
    repeat = hot(iota((128, TERMS), 0) == lax.rem(iota((128, TERMS), 1), PADDED))
    same = iota((TERMS, TERMS), 0) // PADDED == iota((TERMS, TERMS), 1) // PADDED
    high, low = split(coupled[...])
    cbh[...] = jnp.where(same, mm(high, repeat), 0.0).astype(bf16)
    cbl[...] = jnp.where(same, mm(low, repeat), 0.0).astype(bf16)

    def told(k):
        label_from(peer(k + 1)).wait()

    loop(PARTS - 1, told)
    number = lax.rem(iota((128, ROWS), 1), WIDE)
    named = mm(lab_in[...].reshape(PARTS * 8, 128).astype(bf16), hot(iota((128, ROWS), 0) == number))
    source = iota((PARTS * 8, ROWS), 1) // WIDE
    atom = jnp.sum(jnp.where(iota((PARTS * 8, ROWS), 0) == source * 8, named, 0.0), axis=0, keepdims=True)
    number = lax.rem(iota((1, ROWS), 1), WIDE)
    key = jnp.where(atom < 0.0, -1, atom.astype(i32) * PADDED + lax.rem(number, PROJ))
    for i in range(ROWS // BLOCK):
        at = slice(i * BLOCK, (i + 1) * BLOCK)
        mask = jnp.where(iota((TERMS, BLOCK), 0) == key[:, at], 1.0, 0.0)
        member[:, at] = mask.astype(bf16)
        memt[at, :] = mask.T.astype(bf16)

    def face_copy(step, low, other):
        source = face_out.at[pl.ds(0 if low else FACE, FACE)]
        target = face_in.at[step, pl.ds(FACE if low else 0, FACE)]
        side = 0 if low else 1
        return pltpu.make_async_remote_copy(
            source, target, sf.at[side], rf.at[step, 1 - side], device_id=(band, other), device_id_type=MESH
        )

    def face_wait(step, low, other):
        source = face_out.at[pl.ds(0 if low else FACE, FACE)]
        target = face_in.at[step, pl.ds(0 if low else FACE, FACE)]
        side = 0 if low else 1
        return pltpu.make_async_remote_copy(
            source, target, sf.at[side], rf.at[step, side], device_id=(band, other), device_id_type=MESH
        )

    def degree(step):
        gain = jnp.where(step == 0, 1.0, 2.0) / half
        keep = jnp.where(step == 0, 0.0, 1.0)

        def pick(c):
            at = rows_at(c, CELL)
            gh[at, :] = mm(gat[at, :], vh[...]).astype(bf16)
            gl[at, :] = mm(gat[at, :], vl[...]).astype(bf16)
            high, low = split(cell_ham[c])
            high, low = split(mm(high, gh[at, :]) + (mm(high, gl[at, :]) + mm(low, gh[at, :])))
            ph[at, :] = high
            plo[at, :] = low

        loop(CELLS, pick)

        def add(i):
            at = rows_at(i, 512)
            cells[at, :] = mm(sca[at, :], ph[...]) + mm(sca[at, :], plo[...])

        loop(NODES // 512, add)
        high, low = split(cells[...])
        gh[0:NODES, :] = high
        gl[0:NODES, :] = low
        face_out[...] = mm(fgat[...], gh[0:NODES, :]) + mm(fgat[...], gl[0:NODES, :])

        @pl.when(me > 0)
        def _():
            face_copy(step, True, me - 1).start()

        @pl.when(me < PARTS - 1)
        def _():
            face_copy(step, False, me + 1).start()

        for h in range(2):
            collect(h, out1, in1, s1, r1)
            high, low = split(mm(member[...], xh[...]) + mm(member[...], xl[...]))
            applied = mm(cbh[...], high) + (mm(cbh[...], low) + mm(cbl[...], high))
            high, low = split(applied)

            @pl.when(step > 0)
            def _():
                sent(h, out2, in2, s2, r2)

            exchange(h, lambda at: mm(memt[at, :], high) + mm(memt[at, :], low), out2, in2, s2, r2)

        @pl.when(me > 0)
        def _():
            face_wait(step, True, me - 1).wait()

        @pl.when(me < PARTS - 1)
        def _():
            face_wait(step, False, me + 1).wait()

        high, low = split(face_in[step])
        gh[0 : 2 * FACE, :] = high
        gl[0 : 2 * FACE, :] = low

        def assemble(i):
            at = rows_at(i, 512)
            summed = cells[at, :] + mm(fsca[at, :], gh[0:256, :]) + mm(fsca[at, :], gl[0:256, :])
            field = filtered[at, :]
            cells[at, :] = (summed - centre * field) * gain - keep * previous[at, :]
            previous[at, :] = field

        loop(NODES // 512, assemble)
        for h in range(2):
            columns = sides(h)
            collect(h, out2, in2, s2, r2)
            bh, bl = split(mm(placet[...], xh[...]) + mm(placet[...], xl[...]))

            def finish(i):
                at = rows_at(i, 512)
                back = mm(b24th[at, :], bh) + (mm(b24th[at, :], bl) + mm(b24tl[at, :], bh))
                field = cells[at, columns] + gain * back
                filtered[at, columns] = field
                high, low = split(field)
                vh[at, columns] = high
                vl[at, columns] = low

            loop(NODES // 512, finish)
            sent(h, out1, in1, s1, r1)

            @pl.when(step < 2)
            def _():
                send_coefficients(h)

    loop(3, degree)
    for h in range(2):
        sent(h, out2, in2, s2, r2)
    margin_of(
        me, band, other, quarter, node_weight, filtered, margin, vh, vl, wth, wtl, halves, kept, given, core_in, strips,
        turned, swapped, sh, rh, sc, rc, ss, rs, sw, rw,
    )


def margin_of(
    me, band, other, quarter, node_weight, filtered, margin, vh, vl, wth, wtl, halves, kept, given, core_in, strips,
    turned, swapped, sh, rh, sc, rc, ss, rs, sw, rw,
):
    y, x = band // 2, lax.rem(band, 2)
    core, chip = lax.rem(me, 2), me // 2
    sibling = me + 1 - 2 * core
    steps = (
        (0, 1, x, 1 - x),
        (1, 0, 0, 0),
        (3, 0, 1, 1),
        (1, 1, 0, 0),
        (3, 1, 1, 1),
        (2, 0, y // 2, 1 - y // 2),
        (2, 1, y // 2, 1 - y // 2),
    )

    def group_at(dy, dx):
        return lax.rem(y + dy, 4) * 2 + lax.rem(x + dx, 2)

    def half_copy(i):
        dy, dx, mine, _ = steps[i]
        return pltpu.make_async_remote_copy(
            filtered.at[rows_at(mine, NODES // 2)],
            halves.at[i],
            sh.at[i],
            rh.at[i],
            device_id=(group_at(dy, dx), me),
            device_id_type=MESH,
        )

    def core_copy(i):
        return pltpu.make_async_remote_copy(
            given.at[i], core_in.at[i], sc.at[i], rc.at[i], device_id=(band, sibling), device_id_type=MESH
        )

    def strip_copy(i, j, target):
        return pltpu.make_async_remote_copy(
            kept.at[i, j], strips.at[chip], ss.at[i, j], rs.at[chip], device_id=(band, target), device_id_type=MESH
        )

    for i in range(7):
        half_copy(i).start()
    for i in range(NODES // BLOCK):
        at = slice(i * BLOCK, (i + 1) * BLOCK)
        high, low = split(filtered[at, :].T * node_weight[:, at])
        wth[:, at] = high
        wtl[:, at] = low
    lower = iota((128, 128), 1) < 64
    owners = [band] + [group_at((4 - dy) % 4, dx) for dy, dx, _, _ in steps]

    def send_strips(i):
        core_copy(i).wait_recv()
        for j in range(2):
            kept[i, j] = kept[i, j] + core_in[i, j]
            target = owners[i] * 4 + 2 * j + core

            @pl.when(target == me)
            def _():
                strips[chip] = kept[i, j]

            @pl.when(target != me)
            def _():
                strip_copy(i, j, target).start()

    for i in range(GROUPS):
        if i == 0:
            product = mm(wth[...], vh[...]) + (mm(wth[...], vl[...]) + mm(wtl[...], vh[...]))
        else:
            half_copy(i - 1).wait_recv()
            at = rows_at(steps[i - 1][3], NODES // 2)
            high, low = split(halves[i - 1])
            product = mm(wth[:, at], high) + (mm(wth[:, at], low) + mm(wtl[:, at], high))
        for j in range(2):
            top, bottom = product[:128, j * 128 : (j + 1) * 128], product[128:, j * 128 : (j + 1) * 128]
            even = jnp.where(lower, top, pltpu.roll(bottom, 64, 1))
            odd = jnp.where(lower, pltpu.roll(top, 64, 1), bottom)
            kept[i, j] = jnp.where(core == 0, even, odd)
            given[i, j] = jnp.where(core == 0, odd, even)
        core_copy(i).start()
        if i > 0:
            send_strips(i - 1)
    send_strips(GROUPS - 1)

    def arrived(k):
        source = lax.rem(chip + k + 1, PARTS // 2)
        pltpu.make_async_remote_copy(
            kept.at[0, 0], strips.at[source], ss.at[0, 0], rs.at[source], device_id=(band, source * 2 + core), device_id_type=MESH
        ).wait_recv()

    loop(PARTS // 2 - 1, arrived)
    total = jnp.sum(strips[...], axis=0)
    flipped = total.T
    margin[:, :128] = flipped[:64]
    margin[:, 128:] = flipped[64:]

    def swap_copy(j):
        return pltpu.make_async_remote_copy(
            turned.at[pl.ds(64 * (j % 2), 64)],
            swapped.at[quarter],
            sw.at[j],
            rw.at[quarter],
            device_id=(other, band * 4 + j),
            device_id_type=MESH,
        )

    @pl.when(other != band)
    def _():
        turned[...] = total
        for j in range(4):
            swap_copy(j).start()
        for j in range(4):
            pltpu.make_async_remote_copy(
                turned.at[pl.ds(0, 64)], swapped.at[j], sw.at[j], rw.at[j], device_id=(other, band * 4 + j), device_id_type=MESH
            ).wait_recv()
        lowest = iota((64, 128), 1) < 64
        for j in range(2):
            even, odd = swapped[2 * j], swapped[2 * j + 1]
            left = jnp.where(lowest, even, pltpu.roll(odd, 64, 1))
            right = jnp.where(lowest, pltpu.roll(even, 64, 1), odd)
            margin[:, j * 128 : (j + 1) * 128] += jnp.where(quarter < 2, left, right)
        for j in range(4):
            swap_copy(j).wait_send()

    for i in range(7):
        half_copy(i).wait_send()
    for i in range(GROUPS):
        core_copy(i).wait_send()
        for j in range(2):
            target = owners[i] * 4 + 2 * j + core

            @pl.when(target != me)
            def _():
                strip_copy(i, j, target).wait_send()


def run_filter(
    bands_in, cell_ham, cell_nodes, left_face, right_face, proj_values, proj_nodes, slot_owner, slot_atom, coupling, node_weight,
    filter_center, filter_half,
):
    vmem = pl.BlockSpec(memory_space=pltpu.VMEM)
    smem = pl.BlockSpec(memory_space=pltpu.SMEM)
    D = pltpu.SemaphoreType.DMA
    V = pltpu.VMEM
    slot_rows = SLOTS * PADDED
    pairs = D((2, PARTS))
    filtered, margin = pl.pallas_call(
        filter_kernel,
        out_shape=(jax.ShapeDtypeStruct((NODES, COLS), f32), jax.ShapeDtypeStruct((64, COLS), f32)),
        in_specs=[smem] * 2 + [vmem] * 11,
        out_specs=(vmem, vmem),
        scratch_shapes=[
            V((slot_rows, 128), f32),
            V((TERMS, 128), f32),
            V((slot_rows, NODES), f32),
            V((slot_rows, NODES), bf16),
            V((slot_rows, NODES), bf16),
            V((NODES, slot_rows), bf16),
            V((NODES, slot_rows), bf16),
            V((ROWS, slot_rows), bf16),
            V((slot_rows, ROWS), bf16),
            V((CELLS * CELL, NODES), bf16),
            V((NODES, CELLS * CELL), bf16),
            V((2 * FACE, NODES), bf16),
            V((NODES, 2 * FACE), bf16),
            V((TERMS, ROWS), bf16),
            V((ROWS, TERMS), bf16),
            V((TERMS, TERMS), bf16),
            V((TERMS, TERMS), bf16),
            V((NODES, COLS), bf16),
            V((NODES, COLS), bf16),
            V((ROWS, 128), bf16),
            V((ROWS, 128), bf16),
            V((CELLS * CELL, COLS), bf16),
            V((CELLS * CELL, COLS), bf16),
            V((CELLS * CELL, COLS), bf16),
            V((CELLS * CELL, COLS), bf16),
            V((NODES, COLS), f32),
            V((NODES, COLS), f32),
            V((2, PARTS, WIDE, 128), f32),
            V((2, PARTS, WIDE, 128), f32),
            V((2, PARTS, WIDE, 128), f32),
            V((2, PARTS, WIDE, 128), f32),
            V((PARTS, 8, 128), f32),
            V((PARTS, 8, 128), f32),
            V((2 * FACE, COLS), f32),
            V((3, 2 * FACE, COLS), f32),
            pairs,
            pairs,
            pairs,
            pairs,
            D((PARTS,)),
            D((PARTS,)),
            D((2,)),
            D((3, 2)),
            V((COLS, NODES), bf16),
            V((COLS, NODES), bf16),
            V((7, NODES // 2, COLS), f32),
            V((GROUPS, 2, 128, 128), f32),
            V((GROUPS, 2, 128, 128), f32),
            V((GROUPS, 2, 128, 128), f32),
            V((PARTS // 2, 128, 128), f32),
            V((128, 128), f32),
            V((4, 64, 128), f32),
            D((7,)),
            D((7,)),
            D((GROUPS,)),
            D((GROUPS,)),
            D((GROUPS, 2)),
            D((PARTS // 2,)),
            D((4,)),
            D((4,)),
        ],
        compiler_params=pltpu.CompilerParams(
            collective_id=0, has_side_effects=True, vmem_limit_bytes=58 * 2**20
        ),
        name="filter_bands",
    )(
        filter_center,
        filter_half,
        bands_in,
        cell_ham,
        cell_nodes,
        left_face,
        right_face,
        jnp.transpose(proj_values, (1, 0, 2)),
        proj_nodes,
        slot_owner.reshape(1, SLOTS),
        slot_atom.reshape(1, SLOTS),
        jnp.transpose(coupling, (1, 0, 2)),
        node_weight.reshape(1, NODES),
    )
    return filtered, margin.T


def per_device(
    bands_in,
    cell_ham,
    cell_nodes,
    left_face,
    right_face,
    proj_values,
    proj_nodes,
    slot_owner,
    slot_atom,
    coupling,
    node_weight,
    filter_center,
    filter_half,
):
    return run_filter(
        bands_in, cell_ham, cell_nodes, left_face, right_face, proj_values, proj_nodes, slot_owner, slot_atom, coupling,
        node_weight, filter_center, filter_half,
    )


def solution(mesh):
    placed = (
        P("mesh", "band"),
        P("mesh", None, None),
        P("mesh", None),
        P("mesh", None),
        P("mesh", None),
        P("mesh", None, None),
        P("mesh", None),
        P("mesh", None),
        P("mesh"),
        P("mesh", None, None),
        P("mesh"),
        P(),
        P(),
    )
    return jax.shard_map(
        per_device,
        mesh=mesh,
        in_specs=placed,
        out_specs=(P("mesh", "band"), P("band", "mesh")),
        check_vma=False,
    )
```

time: 322 us -> 294 us (0.913)
  Pallas kernels: 298 us -> 285 us
  local copies, waits for them, and re-layouts: 15.1 us -> 3.73 us
  other arithmetic: 3.22 us -> 0 us
    pallas_call x1, Pallas kernels: 298 us -> 285 us  [run_filter(): pl.pallas_call(filter_kernel, out_shape=(jax.ShapeDtypeStruct((NODES, COL...]
    unnamed x8 -> x2, local copies, waits for them, and re-layouts: 8.75 us -> 3.73 us
where the time goes in v3:
time: 294 us; the launch traced here: 291 us
  Pallas kernels  285 us (97%)
  local copies, waits for them, and re-layouts  3.73 us (1%)
    pallas_call x1, Pallas kernels, run_filter(): pl.pallas_call(filter_kernel, out_shape=(jax.ShapeDtypeStruct((NODES, COL...  285 us

profile of v3, /device:TPU:249, one launch (start us, length us, event | category | flops | bytes accessed | tf_op | source)
XLA Modules:
  0.0 290.6 jit_solution(12236264250930353824)
XLA Ops:
  1.9 284.9 %filter_bands.1 = (f32[1024,256]{1,0:T(8,128)}, f32[64,256]{1,0:T(8,128)}) custom-call(f32[1]{0:T(128)S(6)} %copy.17.centre_ref, f32[1]{0:T(128)S(6)} %copy.18.half_ref, f32[1024,256]{1,0:T(8,128)} %bands_in.1, f32[3,512,512]{2,1,0:T(8,128)} %cell_ham.1, s32[3,512]{1,0:T(4,128)} %cell_nodes.1, s32[1,128]{1,0:T(1,128)} %left_face.1, s32[1,128]{1,0:T(1,128)} %right_face.1, ...), custom_call_target="tpu_custom_call" | custom-call | tf_op jit(solution)/shard_map/filter_bands/pallas_call | solution.py:604
  286.8 2.3 copy.19
  289.1 1.5 copy.20

commit v4 on v3

--- a/solution.py
+++ b/solution.py
@@ -115,6 +115,7 @@
     rf,
     wth,
     wtl,
+    product,
     halves,
     kept,
     given,
@@ -450,39 +451,47 @@
     for h in range(2):
         sent(h, out2, in2, s2, r2)
     margin_of(
-        me, band, other, quarter, node_weight, filtered, margin, vh, vl, wth, wtl, halves, kept, given, core_in, strips,
+        me, band, other, quarter, node_weight, filtered, margin, vh, vl, wth, wtl, product, halves, kept, given, core_in, strips,
         turned, swapped, sh, rh, sc, rc, ss, rs, sw, rw,
     )
 
 
 def margin_of(
-    me, band, other, quarter, node_weight, filtered, margin, vh, vl, wth, wtl, halves, kept, given, core_in, strips,
+    me, band, other, quarter, node_weight, filtered, margin, vh, vl, wth, wtl, product, halves, kept, given, core_in, strips,
     turned, swapped, sh, rh, sc, rc, ss, rs, sw, rw,
 ):
     y, x = band // 2, lax.rem(band, 2)
     core, chip = lax.rem(me, 2), me // 2
     sibling = me + 1 - 2 * core
-    steps = (
-        (0, 1, x, 1 - x),
-        (1, 0, 0, 0),
-        (3, 0, 1, 1),
-        (1, 1, 0, 0),
-        (3, 1, 1, 1),
-        (2, 0, y // 2, 1 - y // 2),
-        (2, 1, y // 2, 1 - y // 2),
-    )
+    far = y // 2
+
+    def choose(i, values):
+        result = values[0]
+        for k in range(1, GROUPS):
+            result = jnp.where(i == k, values[k], result)
+        return result
+
+    def block_at(t):
+        return lax.rem(t + chip, GROUPS)
 
     def group_at(dy, dx):
         return lax.rem(y + dy, 4) * 2 + lax.rem(x + dx, 2)
 
+    def apart(i):
+        return choose(i, (0, 0, 1, 3, 1, 3, 2, 2)), choose(i, (0, 1, 0, 0, 1, 1, 0, 1))
+
+    def owner(i):
+        dy, dx = apart(i)
+        return group_at(4 - dy, dx)
+
     def half_copy(i):
-        dy, dx, mine, _ = steps[i]
+        mine = choose(i, (0, x, 0, 1, 0, 1, far, far))
         return pltpu.make_async_remote_copy(
             filtered.at[rows_at(mine, NODES // 2)],
-            halves.at[i],
-            sh.at[i],
-            rh.at[i],
-            device_id=(group_at(dy, dx), me),
+            halves.at[i - 1],
+            sh.at[i - 1],
+            rh.at[i - 1],
+            device_id=(group_at(*apart(i)), me),
             device_id_type=MESH,
         )
 
@@ -496,21 +505,26 @@
             kept.at[i, j], strips.at[chip], ss.at[i, j], rs.at[chip], device_id=(band, target), device_id_type=MESH
         )
 
-    for i in range(7):
-        half_copy(i).start()
+    def begin(t):
+        i = block_at(t)
+
+        @pl.when(i > 0)
+        def _():
+            half_copy(i).start()
+
+    loop(GROUPS, begin)
     for i in range(NODES // BLOCK):
         at = slice(i * BLOCK, (i + 1) * BLOCK)
         high, low = split(filtered[at, :].T * node_weight[:, at])
         wth[:, at] = high
         wtl[:, at] = low
     lower = iota((128, 128), 1) < 64
-    owners = [band] + [group_at((4 - dy) % 4, dx) for dy, dx, _, _ in steps]
 
     def send_strips(i):
         core_copy(i).wait_recv()
         for j in range(2):
             kept[i, j] = kept[i, j] + core_in[i, j]
-            target = owners[i] * 4 + 2 * j + core
+            target = owner(i) * 4 + 2 * j + core
 
             @pl.when(target == me)
             def _():
@@ -520,14 +534,20 @@
             def _():
                 strip_copy(i, j, target).start()
 
-    for i in range(GROUPS):
-        if i == 0:
-            product = mm(wth[...], vh[...]) + (mm(wth[...], vl[...]) + mm(wtl[...], vh[...]))
-        else:
-            half_copy(i - 1).wait_recv()
-            at = rows_at(steps[i - 1][3], NODES // 2)
+    def multiply(t):
+        i = block_at(t)
+
+        @pl.when(i == 0)
+        def _():
+            product[...] = mm(wth[...], vh[...]) + (mm(wth[...], vl[...]) + mm(wtl[...], vh[...]))
+
+        @pl.when(i > 0)
+        def _():
+            half_copy(i).wait_recv()
+            at = rows_at(choose(i, (0, 1 - x, 0, 1, 0, 1, 1 - far, 1 - far)), NODES // 2)
             high, low = split(halves[i - 1])
-            product = mm(wth[:, at], high) + (mm(wth[:, at], low) + mm(wtl[:, at], high))
+            product[...] = mm(wth[:, at], high) + (mm(wth[:, at], low) + mm(wtl[:, at], high))
+
         for j in range(2):
             top, bottom = product[:128, j * 128 : (j + 1) * 128], product[128:, j * 128 : (j + 1) * 128]
             even = jnp.where(lower, top, pltpu.roll(bottom, 64, 1))
@@ -535,9 +555,13 @@
             kept[i, j] = jnp.where(core == 0, even, odd)
             given[i, j] = jnp.where(core == 0, odd, even)
         core_copy(i).start()
-        if i > 0:
-            send_strips(i - 1)
-    send_strips(GROUPS - 1)
+
+        @pl.when(t > 0)
+        def _():
+            send_strips(block_at(t + GROUPS - 1))
+
+    loop(GROUPS, multiply)
+    send_strips(block_at(GROUPS - 1))
 
     def arrived(k):
         source = lax.rem(chip + k + 1, PARTS // 2)
@@ -579,16 +603,20 @@
         for j in range(4):
             swap_copy(j).wait_send()
 
-    for i in range(7):
-        half_copy(i).wait_send()
-    for i in range(GROUPS):
+    def finished(i):
+        @pl.when(i > 0)
+        def _():
+            half_copy(i).wait_send()
+
         core_copy(i).wait_send()
         for j in range(2):
-            target = owners[i] * 4 + 2 * j + core
+            target = owner(i) * 4 + 2 * j + core
 
             @pl.when(target != me)
             def _():
                 strip_copy(i, j, target).wait_send()
+
+    loop(GROUPS, finished)
 
 
 def run_filter(
@@ -652,6 +680,7 @@
             D((3, 2)),
             V((COLS, NODES), bf16),
             V((COLS, NODES), bf16),
+            V((COLS, COLS), f32),
             V((7, NODES // 2, COLS), f32),
             V((GROUPS, 2, 128, 128), f32),
             V((GROUPS, 2, 128, 128), f32),

time: 294 us -> 288 us (0.980); the launches traced: 291 us -> 288 us
  no operation moved by 1% of the time
where the time goes in v4:
time: 288 us
  Pallas kernels  283 us (98%)
  local copies, waits for them, and re-layouts  3.73 us (1%)
    pallas_call x1, Pallas kernels, run_filter(): pl.pallas_call(filter_kernel, out_shape=(jax.ShapeDtypeStruct((NODES, COL...  283 us

profile of v4, /device:TPU:249, one launch (start us, length us, event | category | flops | bytes accessed | tf_op | source)
XLA Modules:
  0.0 288.3 jit_solution(15922497971356188292)
XLA Ops:
  1.9 282.6 %filter_bands.1 = (f32[1024,256]{1,0:T(8,128)}, f32[64,256]{1,0:T(8,128)}) custom-call(f32[1]{0:T(128)S(6)} %copy.17.centre_ref, f32[1]{0:T(128)S(6)} %copy.18.half_ref, f32[1024,256]{1,0:T(8,128)} %bands_in.1, f32[3,512,512]{2,1,0:T(8,128)} %cell_ham.1, s32[3,512]{1,0:T(4,128)} %cell_nodes.1, s32[1,128]{1,0:T(1,128)} %left_face.1, s32[1,128]{1,0:T(1,128)} %right_face.1, ...), custom_call_target="tpu_custom_call" | custom-call | tf_op jit(solution)/shard_map/filter_bands/pallas_call | solution.py:632
  284.5 2.3 copy.19
  286.8 1.5 copy.20

commit v5 on v4

--- a/solution.py
+++ b/solution.py
@@ -447,6 +447,22 @@
             def _():
                 send_coefficients(h)
 
+            @pl.when(step == 2)
+            def _():
+                def begin(t):
+                    i = lax.rem(t + me // 2, GROUPS)
+
+                    @pl.when(i > 0)
+                    def _():
+                        half_of(i, h, me, band, filtered, halves, sh, rh).start()
+
+                loop(GROUPS, begin)
+                for i in range(NODES // BLOCK):
+                    at = slice(i * BLOCK, (i + 1) * BLOCK)
+                    high, low = split(filtered[at, columns].T * node_weight[:, at])
+                    wth[columns, at] = high
+                    wtl[columns, at] = low
+
     loop(3, degree)
     for h in range(2):
         sent(h, out2, in2, s2, r2)
@@ -456,44 +472,52 @@
     )
 
 
+def choose(i, values):
+    result = values[0]
+    for k in range(1, GROUPS):
+        result = jnp.where(i == k, values[k], result)
+    return result
+
+
+def apart(i):
+    return choose(i, (0, 0, 1, 3, 1, 3, 2, 2)), choose(i, (0, 1, 0, 0, 1, 1, 0, 1))
+
+
+def group_at(band, dy, dx):
+    return lax.rem(band // 2 + dy, 4) * 2 + lax.rem(band + dx, 2)
+
+
+def half_of(i, h, me, band, filtered, halves, sh, rh):
+    x, far = lax.rem(band, 2), band // 4
+    mine = choose(i, (0, x, 0, 1, 0, 1, far, far))
+    columns = pl.ds(h * 128, 128)
+    return pltpu.make_async_remote_copy(
+        filtered.at[rows_at(mine, NODES // 2), columns],
+        halves.at[i - 1, :, columns],
+        sh.at[i - 1, h],
+        rh.at[i - 1, h],
+        device_id=(group_at(band, *apart(i)), me),
+        device_id_type=MESH,
+    )
+
+
 def margin_of(
     me, band, other, quarter, node_weight, filtered, margin, vh, vl, wth, wtl, product, halves, kept, given, core_in, strips,
     turned, swapped, sh, rh, sc, rc, ss, rs, sw, rw,
 ):
-    y, x = band // 2, lax.rem(band, 2)
+    x, far = lax.rem(band, 2), band // 4
     core, chip = lax.rem(me, 2), me // 2
     sibling = me + 1 - 2 * core
-    far = y // 2
-
-    def choose(i, values):
-        result = values[0]
-        for k in range(1, GROUPS):
-            result = jnp.where(i == k, values[k], result)
-        return result
 
     def block_at(t):
         return lax.rem(t + chip, GROUPS)
 
-    def group_at(dy, dx):
-        return lax.rem(y + dy, 4) * 2 + lax.rem(x + dx, 2)
-
-    def apart(i):
-        return choose(i, (0, 0, 1, 3, 1, 3, 2, 2)), choose(i, (0, 1, 0, 0, 1, 1, 0, 1))
-
     def owner(i):
         dy, dx = apart(i)
-        return group_at(4 - dy, dx)
-
-    def half_copy(i):
-        mine = choose(i, (0, x, 0, 1, 0, 1, far, far))
-        return pltpu.make_async_remote_copy(
-            filtered.at[rows_at(mine, NODES // 2)],
-            halves.at[i - 1],
-            sh.at[i - 1],
-            rh.at[i - 1],
-            device_id=(group_at(*apart(i)), me),
-            device_id_type=MESH,
-        )
+        return group_at(band, 4 - dy, dx)
+
+    def half_copy(i, h):
+        return half_of(i, h, me, band, filtered, halves, sh, rh)
 
     def core_copy(i):
         return pltpu.make_async_remote_copy(
@@ -505,19 +529,6 @@
             kept.at[i, j], strips.at[chip], ss.at[i, j], rs.at[chip], device_id=(band, target), device_id_type=MESH
         )
 
-    def begin(t):
-        i = block_at(t)
-
-        @pl.when(i > 0)
-        def _():
-            half_copy(i).start()
-
-    loop(GROUPS, begin)
-    for i in range(NODES // BLOCK):
-        at = slice(i * BLOCK, (i + 1) * BLOCK)
-        high, low = split(filtered[at, :].T * node_weight[:, at])
-        wth[:, at] = high
-        wtl[:, at] = low
     lower = iota((128, 128), 1) < 64
 
     def send_strips(i):
@@ -543,7 +554,8 @@
 
         @pl.when(i > 0)
         def _():
-            half_copy(i).wait_recv()
+            for h in range(2):
+                half_copy(i, h).wait_recv()
             at = rows_at(choose(i, (0, 1 - x, 0, 1, 0, 1, 1 - far, 1 - far)), NODES // 2)
             high, low = split(halves[i - 1])
             product[...] = mm(wth[:, at], high) + (mm(wth[:, at], low) + mm(wtl[:, at], high))
@@ -606,7 +618,8 @@
     def finished(i):
         @pl.when(i > 0)
         def _():
-            half_copy(i).wait_send()
+            for h in range(2):
+                half_copy(i, h).wait_send()
 
         core_copy(i).wait_send()
         for j in range(2):
@@ -688,8 +701,8 @@
             V((PARTS // 2, 128, 128), f32),
             V((128, 128), f32),
             V((4, 64, 128), f32),
-            D((7,)),
-            D((7,)),
+            D((7, 2)),
+            D((7, 2)),
             D((GROUPS,)),
             D((GROUPS,)),
             D((GROUPS, 2)),

time: 288 us -> 281 us (0.976)
  Pallas kernels: 283 us -> 275 us
    pallas_call x1, Pallas kernels: 283 us -> 275 us  [run_filter(): pl.pallas_call(filter_kernel, out_shape=(jax.ShapeDtypeStruct((NODES, COL...]
where the time goes in v5:
time: 281 us
  Pallas kernels  275 us (98%)
  local copies, waits for them, and re-layouts  3.73 us (1%)
    pallas_call x1, Pallas kernels, run_filter(): pl.pallas_call(filter_kernel, out_shape=(jax.ShapeDtypeStruct((NODES, COL...  275 us

profile of v5, /device:TPU:249, one launch (start us, length us, event | category | flops | bytes accessed | tf_op | source)
XLA Modules:
  0.0 280.6 jit_solution(10799577472466729825)
XLA Ops:
  1.9 274.9 %filter_bands.1 = (f32[1024,256]{1,0:T(8,128)}, f32[64,256]{1,0:T(8,128)}) custom-call(f32[1]{0:T(128)S(6)} %copy.17.centre_ref, f32[1]{0:T(128)S(6)} %copy.18.half_ref, f32[1024,256]{1,0:T(8,128)} %bands_in.1, f32[3,512,512]{2,1,0:T(8,128)} %cell_ham.1, s32[3,512]{1,0:T(4,128)} %cell_nodes.1, s32[1,128]{1,0:T(1,128)} %left_face.1, s32[1,128]{1,0:T(1,128)} %right_face.1, ...), custom_call_target="tpu_custom_call" | custom-call | tf_op jit(solution)/shard_map/filter_bands/pallas_call | solution.py:645
  276.8 2.3 copy.19
  279.1 1.5 copy.20

commit v6 on v5

--- a/solution.py
+++ b/solution.py
@@ -519,9 +519,9 @@
     def half_copy(i, h):
         return half_of(i, h, me, band, filtered, halves, sh, rh)
 
-    def core_copy(i):
-        return pltpu.make_async_remote_copy(
-            given.at[i], core_in.at[i], sc.at[i], rc.at[i], device_id=(band, sibling), device_id_type=MESH
+    def core_copy(i, j):
+        return pltpu.make_async_remote_copy(
+            given.at[i, j], core_in.at[i, j], sc.at[i, j], rc.at[i, j], device_id=(band, sibling), device_id_type=MESH
         )
 
     def strip_copy(i, j, target):
@@ -531,49 +531,49 @@
 
     lower = iota((128, 128), 1) < 64
 
-    def send_strips(i):
-        core_copy(i).wait_recv()
-        for j in range(2):
-            kept[i, j] = kept[i, j] + core_in[i, j]
-            target = owner(i) * 4 + 2 * j + core
-
-            @pl.when(target == me)
-            def _():
-                strips[chip] = kept[i, j]
-
-            @pl.when(target != me)
-            def _():
-                strip_copy(i, j, target).start()
-
-    def multiply(t):
+    def send_strips(i, j):
+        core_copy(i, j).wait_recv()
+        kept[i, j] = kept[i, j] + core_in[i, j]
+        target = owner(i) * 4 + 2 * j + core
+
+        @pl.when(target == me)
+        def _():
+            strips[chip] = kept[i, j]
+
+        @pl.when(target != me)
+        def _():
+            strip_copy(i, j, target).start()
+
+    def multiply(t, j):
         i = block_at(t)
+        columns = slice(j * 128, (j + 1) * 128)
 
         @pl.when(i == 0)
         def _():
-            product[...] = mm(wth[...], vh[...]) + (mm(wth[...], vl[...]) + mm(wtl[...], vh[...]))
+            high, low = vh[:, columns], vl[:, columns]
+            product[...] = mm(wth[...], high) + (mm(wth[...], low) + mm(wtl[...], high))
 
         @pl.when(i > 0)
         def _():
-            for h in range(2):
-                half_copy(i, h).wait_recv()
+            half_copy(i, j).wait_recv()
             at = rows_at(choose(i, (0, 1 - x, 0, 1, 0, 1, 1 - far, 1 - far)), NODES // 2)
-            high, low = split(halves[i - 1])
+            high, low = split(halves[i - 1, :, columns])
             product[...] = mm(wth[:, at], high) + (mm(wth[:, at], low) + mm(wtl[:, at], high))
 
-        for j in range(2):
-            top, bottom = product[:128, j * 128 : (j + 1) * 128], product[128:, j * 128 : (j + 1) * 128]
-            even = jnp.where(lower, top, pltpu.roll(bottom, 64, 1))
-            odd = jnp.where(lower, pltpu.roll(top, 64, 1), bottom)
-            kept[i, j] = jnp.where(core == 0, even, odd)
-            given[i, j] = jnp.where(core == 0, odd, even)
-        core_copy(i).start()
+        top, bottom = product[:128, :], product[128:, :]
+        even = jnp.where(lower, top, pltpu.roll(bottom, 64, 1))
+        odd = jnp.where(lower, pltpu.roll(top, 64, 1), bottom)
+        kept[i, j] = jnp.where(core == 0, even, odd)
+        given[i, j] = jnp.where(core == 0, odd, even)
+        core_copy(i, j).start()
 
         @pl.when(t > 0)
         def _():
-            send_strips(block_at(t + GROUPS - 1))
-
-    loop(GROUPS, multiply)
-    send_strips(block_at(GROUPS - 1))
+            send_strips(block_at(t + GROUPS - 1), j)
+
+    for j in range(2):
+        loop(GROUPS, lambda t: multiply(t, j))
+        send_strips(block_at(GROUPS - 1), j)
 
     def arrived(k):
         source = lax.rem(chip + k + 1, PARTS // 2)
@@ -621,8 +621,8 @@
             for h in range(2):
                 half_copy(i, h).wait_send()
 
-        core_copy(i).wait_send()
         for j in range(2):
+            core_copy(i, j).wait_send()
             target = owner(i) * 4 + 2 * j + core
 
             @pl.when(target != me)
@@ -693,7 +693,7 @@
             D((3, 2)),
             V((COLS, NODES), bf16),
             V((COLS, NODES), bf16),
-            V((COLS, COLS), f32),
+            V((COLS, 128), f32),
             V((7, NODES // 2, COLS), f32),
             V((GROUPS, 2, 128, 128), f32),
             V((GROUPS, 2, 128, 128), f32),
@@ -703,8 +703,8 @@
             V((4, 64, 128), f32),
             D((7, 2)),
             D((7, 2)),
-            D((GROUPS,)),
-            D((GROUPS,)),
+            D((GROUPS, 2)),
+            D((GROUPS, 2)),
             D((GROUPS, 2)),
             D((PARTS // 2,)),
             D((4,)),

time: 281 us -> 277 us (0.986)
  Pallas kernels: 275 us -> 271 us
    pallas_call x1, Pallas kernels: 275 us -> 271 us  [run_filter(): pl.pallas_call(filter_kernel, out_shape=(jax.ShapeDtypeStruct((NODES, COL...]
where the time goes in v6:
time: 277 us
  Pallas kernels  271 us (98%)
  local copies, waits for them, and re-layouts  3.73 us (1%)
    pallas_call x1, Pallas kernels, run_filter(): pl.pallas_call(filter_kernel, out_shape=(jax.ShapeDtypeStruct((NODES, COL...  271 us

profile of v6, /device:TPU:249, one launch (start us, length us, event | category | flops | bytes accessed | tf_op | source)
XLA Modules:
  0.0 276.8 jit_solution(2451711672346730931)
XLA Ops:
  1.9 271.1 %filter_bands.1 = (f32[1024,256]{1,0:T(8,128)}, f32[64,256]{1,0:T(8,128)}) custom-call(f32[1]{0:T(128)S(6)} %copy.17.centre_ref, f32[1]{0:T(128)S(6)} %copy.18.half_ref, f32[1024,256]{1,0:T(8,128)} %bands_in.1, f32[3,512,512]{2,1,0:T(8,128)} %cell_ham.1, s32[3,512]{1,0:T(4,128)} %cell_nodes.1, s32[1,128]{1,0:T(1,128)} %left_face.1, s32[1,128]{1,0:T(1,128)} %right_face.1, ...), custom_call_target="tpu_custom_call" | custom-call | tf_op jit(solution)/shard_map/filter_bands/pallas_call | solution.py:645
  273.1 2.3 copy.19
  275.3 1.5 copy.20
